TPU v7x, 128 devices: a whole 4x4x4 slice. The times are simulated.
128 devices in a mesh: gz: 32 (over x, z_hi, y), gy: 4 (over z_lo, core).
Axes of the slice: x: 4, y: 4, z: 4 (z_hi: 2, z_lo: 2; z = z_hi * 2 + z_lo), core: 2. Of those that a mesh axis runs over, the one named last changes fastest.
Arguments:
- density_field: float32 [4, 64, 256, 256], P(None, 'gz', 'gy'), may hold values from -42 to 42
- first_weight: bfloat16 [54, 128], replicated, may hold values from -0.875 to 0.875
- first_bias: float32 [128], replicated, may hold values from -3 to 3
- middle_weight: bfloat16 [128, 128], replicated, may hold values from -0.5 to 0.5
- middle_bias: float32 [128], replicated, may hold values from -3 to 3
- output_weight: bfloat16 [108, 128], replicated, may hold values from -0.109375 to 0.109375
- output_bias: float32 [4], replicated, may hold values from -3 to 3
- radial_weights: float32 [16, 8, 32], replicated, may hold values from -1 to 1
Outputs:
- factored: float32 [16, 32, 128, 128], P(None, 'gz', 'gy')
- latent: float32 [16, 32, 128, 128], P(None, 'gz', 'gy')
- log_density: float32 [], replicated
All inputs are finite; a program needn't handle non-finite values.
Results may differ from a plain program's by a relative error of at most 0.00065.
The roundings to bfloat16 on the way count: a program that leaves them out, or rounds other values in their place, can miss the bound.
Values may be sent and summed in bfloat16 or wider, within the bound.
A program may use at most 128 MiB of HBM per device.

v0:
```python
import math

import jax
import jax.numpy as jnp
from jax import lax
from jax.sharding import PartitionSpec as P

precise = lax.Precision.HIGHEST


def with_halo(cells, sides, width):
    for axis, dim in sides:
        count = lax.axis_size(axis)
        ends = count - 1
        head = lax.slice_in_dim(cells, 0, width, axis=dim)
        tail = lax.slice_in_dim(cells, cells.shape[dim] - width, cells.shape[dim], axis=dim)
        cells = jnp.concatenate(
            [
                lax.ppermute(tail, axis, [(i, (i + 1) % count) for i in range(ends)]),
                cells,
                lax.ppermute(head, axis, [((i + 1) % count, i) for i in range(ends)]),
            ],
            axis=dim,
        )
    return cells


def fourier_tables(length):
    counting = jnp.arange(length, dtype=jnp.int32)
    product = counting[:, None] * counting[None, :] % length
    phase = product.astype(jnp.float32) * (2.0 * math.pi / length)
    return (jnp.cos(phase), jnp.sin(phase))


def signed_freq(counting, length):
    return (
        jnp.where(2 * counting >= length, counting - length, counting).astype(jnp.float32) / length
    )


def radial_basis(kappa_norm, count_basis):
    centres = jnp.arange(count_basis, dtype=jnp.float32).reshape(
        (count_basis,) + (1,) * kappa_norm.ndim
    )
    scaled = kappa_norm[None] * (count_basis - 1) - centres
    return jnp.exp(-scaled * scaled)


def take_offset(values, offset, along_axis):
    if offset == 1:
        return values
    length = values.shape[along_axis]
    pad_spec = [(0, 0)] * values.ndim
    if offset == 0:
        pad_spec[along_axis] = (1, 0)
        return jnp.pad(lax.slice_in_dim(values, 0, length - 1, axis=along_axis), pad_spec)
    pad_spec[along_axis] = (0, 1)
    return jnp.pad(lax.slice_in_dim(values, 1, length, axis=along_axis), pad_spec)


def hidden_layers(rimmed, first_weight, first_bias, middle_weight, middle_bias):
    out_depth = rimmed.shape[1] - 2
    out_rows = rimmed.shape[2] - 2
    cells_x = rimmed.shape[3]
    padded = jnp.pad(rimmed, ((0, 0), (0, 0), (0, 0), (1, 1)))
    columns = jnp.stack(
        [
            padded[
                channel,
                z_tap : z_tap + out_depth,
                y_tap : y_tap + out_rows,
                x_tap : x_tap + cells_x,
            ]
            for channel in range(2)
            for z_tap in range(3)
            for y_tap in range(3)
            for x_tap in range(3)
        ],
        axis=1,
    )

    def one_plane(plane_columns):
        flat_columns = plane_columns.reshape(54, out_rows * cells_x)
        first_layer = jnp.einsum(
            "kh,kn->hn", first_weight, flat_columns, preferred_element_type=jnp.float32
        )
        first_layer = jax.nn.relu(first_layer + first_bias[:, None]).astype(jnp.bfloat16)
        second_layer = jnp.einsum(
            "kh,kn->hn", middle_weight, first_layer, preferred_element_type=jnp.float32
        )
        second_layer = jax.nn.relu(second_layer + middle_bias[:, None]).astype(jnp.bfloat16)
        return second_layer.reshape(middle_weight.shape[1], out_rows, cells_x)

    return lax.map(one_plane, columns)


def conv_wide(wide, output_weight, local_depth, local_rows):
    raw_affine = 0.0
    for z_tap in range(3):
        projected = jnp.einsum(
            "rh,zhyx->rzyx",
            output_weight[36 * z_tap : 36 * (z_tap + 1)],
            wide[z_tap : z_tap + local_depth],
            preferred_element_type=jnp.float32,
        )
        projected = projected.reshape((3, 3, 4) + projected.shape[1:])
        for y_tap in range(3):
            for x_tap in range(3):
                raw_affine = raw_affine + take_offset(
                    projected[y_tap, x_tap, :, :, y_tap : y_tap + local_rows], x_tap, 3
                )
    return raw_affine


def shards(
    density_field,
    first_weight,
    first_bias,
    middle_weight,
    middle_bias,
    output_weight,
    output_bias,
    radial_weights,
):
    local_depth = density_field.shape[1]
    local_rows = density_field.shape[2]
    local_width = density_field.shape[3]
    count_gz = lax.axis_size("gz")
    count_gy = lax.axis_size("gy")
    lower_half = density_field[0:2].astype(jnp.bfloat16)
    rim_width = 1
    rimmed = with_halo(lower_half, (("gz", 1), ("gy", 2)), rim_width)
    hidden = hidden_layers(rimmed, first_weight, first_bias, middle_weight, middle_bias)
    wide = with_halo(hidden, (("gz", 0), ("gy", 2)), 1)
    raw_affine = conv_wide(wide, output_weight, local_depth, local_rows)
    raw_affine = raw_affine + output_bias[:, None, None, None]
    log_first = jnp.tanh(raw_affine[0:2])
    upper_half = density_field[2:4] * jnp.exp(log_first) + raw_affine[2:4]
    coupled = jnp.concatenate([density_field[0:2], upper_half], axis=0)
    half_z, half_y, half_x = (local_depth // 2, local_rows // 2, local_width // 2)
    squeezed = (
        coupled.reshape(4, half_z, 2, half_y, 2, half_x, 2)
        .transpose(2, 4, 6, 0, 1, 3, 5)
        .reshape(32, half_z, half_y, half_x)
    )
    factored = squeezed[0:16]
    source = squeezed[16:24]
    target = squeezed[24:32]
    first_term = jnp.sum(log_first)
    split_term = -0.5 * jnp.sum(factored * factored)
    early_totals = lax.psum((first_term, split_term), ("gz", "gy"))
    length_z = half_z * count_gz
    length_y = half_y * count_gy
    cos_x, sin_x = fourier_tables(half_x)
    cos_z, sin_z = fourier_tables(length_z)
    cos_y, sin_y = fourier_tables(length_y)
    real_x = jnp.einsum("czyx,xk->cyzk", source, cos_x, precision=precise)
    imag_x = -jnp.einsum("czyx,xk->cyzk", source, sin_x, precision=precise)
    z_pencil = lax.all_to_all(
        jnp.stack([real_x, imag_x]), "gz", split_axis=4, concat_axis=3, tiled=True
    )
    real_z = jnp.einsum("cyzk,zq->cykq", z_pencil[0], cos_z, precision=precise) + jnp.einsum(
        "cyzk,zq->cykq", z_pencil[1], sin_z, precision=precise
    )
    imag_z = jnp.einsum("cyzk,zq->cykq", z_pencil[1], cos_z, precision=precise) - jnp.einsum(
        "cyzk,zq->cykq", z_pencil[0], sin_z, precision=precise
    )
    y_pencil = lax.all_to_all(
        jnp.stack([real_z, imag_z]), "gy", split_axis=4, concat_axis=2, tiled=True
    )
    real_y = jnp.einsum("cykq,yr->ckqr", y_pencil[0], cos_y, precision=precise) + jnp.einsum(
        "cykq,yr->ckqr", y_pencil[1], sin_y, precision=precise
    )
    imag_y = jnp.einsum("cykq,yr->ckqr", y_pencil[1], cos_y, precision=precise) - jnp.einsum(
        "cykq,yr->ckqr", y_pencil[0], sin_y, precision=precise
    )
    modes_x = real_y.shape[1]
    modes_z = real_y.shape[2]
    freq_x = signed_freq(
        lax.axis_index("gz") * modes_x + jnp.arange(modes_x, dtype=jnp.int32), half_x
    )
    freq_z = signed_freq(
        lax.axis_index("gy") * modes_z + jnp.arange(modes_z, dtype=jnp.int32), length_z
    )
    freq_y = signed_freq(jnp.arange(length_y, dtype=jnp.int32), length_y)
    kappa_norm = jnp.sqrt(
        freq_z[None, :, None] ** 2 + freq_y[None, None, :] ** 2 + freq_x[:, None, None] ** 2
    ) * (2.0 / math.sqrt(3.0))
    basis_values = radial_basis(kappa_norm, radial_weights.shape[2])
    profile = jnp.einsum("ocj,jabd->ocabd", radial_weights, basis_values, precision=precise)
    mixed_real = jnp.einsum("ocabd,cabd->oabd", profile, real_y, precision=precise)
    mixed_imag = jnp.einsum("ocabd,cabd->oabd", profile, imag_y, precision=precise)
    back_real = jnp.einsum("oabd,dy->oyab", mixed_real, cos_y, precision=precise) - jnp.einsum(
        "oabd,dy->oyab", mixed_imag, sin_y, precision=precise
    )
    back_imag = jnp.einsum("oabd,dy->oyab", mixed_real, sin_y, precision=precise) + jnp.einsum(
        "oabd,dy->oyab", mixed_imag, cos_y, precision=precise
    )
    y_return = lax.all_to_all(
        jnp.stack([back_real, back_imag]), "gy", split_axis=2, concat_axis=4, tiled=True
    )
    plane_real = jnp.einsum("oyaq,qz->oyza", y_return[0], cos_z, precision=precise) - jnp.einsum(
        "oyaq,qz->oyza", y_return[1], sin_z, precision=precise
    )
    plane_imag = jnp.einsum("oyaq,qz->oyza", y_return[0], sin_z, precision=precise) + jnp.einsum(
        "oyaq,qz->oyza", y_return[1], cos_z, precision=precise
    )
    z_return = lax.all_to_all(
        jnp.stack([plane_real, plane_imag]), "gz", split_axis=3, concat_axis=4, tiled=True
    )
    shifts = jnp.einsum("oyzk,kx->ozyx", z_return[0], cos_x, precision=precise) - jnp.einsum(
        "oyzk,kx->ozyx", z_return[1], sin_x, precision=precise
    )
    shifts = shifts / float(half_x * length_y * length_z)
    log_second = jnp.tanh(shifts[0:8])
    latent = jnp.concatenate([source, target * jnp.exp(log_second) + shifts[8:16]], axis=0)
    second_term = jnp.sum(log_second)
    latent_term = -0.5 * jnp.sum(latent * latent)
    late_totals = lax.psum((second_term, latent_term), ("gz", "gy"))
    whole_sum = early_totals[0] + early_totals[1] + late_totals[0] + late_totals[1]
    cell_count = 4.0 * local_depth * local_rows * local_width * count_gz * count_gy
    log_density = whole_sum / cell_count - 0.5 * math.log(2.0 * math.pi)
    return (factored, latent, log_density)


def solution(mesh):
    in_specs = (P(None, "gz", "gy", None), P(), P(), P(), P(), P(), P(), P())
    out_specs = (P(None, "gz", "gy", None), P(None, "gz", "gy", None), P())
    return jax.shard_map(shards, mesh=mesh, in_specs=in_specs, out_specs=out_specs, check_vma=False)
```

profile of v0, /device:TPU:1, one launch (start us, length us, event | category | flops | bytes accessed | tf_op | source)
XLA Modules:
  0.0 463.4 jit_solution(17733030464298724004)
XLA Ops:
  2.9 4.0 collective-permute-start
  9.0 3.6 collective-permute-done.1
  12.6 5.5 %collective-permute-start.2 = (bf16[2,4,1,256]{3,1,2,0:T(4,128)(2,1)S(1)}, bf16[2,4,1,256]{3,1,2,0:T(4,128)(2,1)S(1)}, u32[]{:S(2)}, u32[]{:S(2)}) collective-permute-start(bf16[2,4,1,256]{3,1,2,0:T(4,128)(2,1)S(1)} %get-tuple-element.140), channel_id=1, source_target_pairs={{0,1},{1,2},{2,3},{4,5},{5,6},{6,7},{8,9},{9,10},{10,11},{12,13},{... | collective-permute-start | bytes 12296 | tf_op jit(solution)/shard_map/ppermute | solution.py:19
  18.2 1.9 collective-permute-start.3
  20.1 3.0 collective-permute-done.3
  31.9 2.5 copy.221
  34.4 36.7 %while.10 = (s32[]{:T(128)}, bf16[2,128,64,256]{3,1,2,0:T(8,128)(2,1)}, bf16[2,54,64,256]{3,2,1,0:T(8,128)(2,1)}, bf16[54,128]{1,0:T(8,128)(2,1)S(1)}, f32[128]{...) while((s32[]{:T(128)}, bf16[2,128,64,256]{3,1,2,0:T(8,128)(2,1)}, ...), condition=%wide.region_1.2_spmd, body=%wide.region_0.1_spmd.sunk | while | flops 775946240 | bytes 33602656 | solution.py:94
  37.5 4.3 fusion.263
  41.9 6.3 %copy.348 = bf16[1,128,64,256]{3,1,2,0:T(8,128)(2,1)} copy(bf16[1,128,64,256]{1,3,2,0:T(8,128)(2,1)} %bitcast.590) | data formatting | bytes 8388608 | tf_op jit(solution)/shard_map/while/body/jit(dynamic_update_index_in_dim)/dynamic_update_slice | solution.py:94
  48.2 4.6 constant_dynamic-update-slice_fusion.59
  55.8 4.3 fusion.263
  60.1 6.3 %copy.348 = bf16[1,128,64,256]{3,1,2,0:T(8,128)(2,1)} copy(bf16[1,128,64,256]{1,3,2,0:T(8,128)(2,1)} %bitcast.590) | data formatting | bytes 8388608 | tf_op jit(solution)/shard_map/while/body/jit(dynamic_update_index_in_dim)/dynamic_update_slice | solution.py:94
  66.5 4.7 %constant_dynamic-update-slice_fusion.59 = bf16[2,128,64,256]{3,1,2,0:T(8,128)(2,1)} fusion(bf16[2,128,64,256]{3,1,2,0:T(8,128)(2,1)} %get-tuple-element.200, bf16[1,128,64,256]{3,1,2,0:T(8,128)(2,1)} %copy.348, s32[]{:T(128)} %get-tuple-element.199), kind=kLoop, calls=%fused_computation.7.clone.1 | loop fusion | bytes 8389120 | tf_op jit(solution)/shard_map/while/body/jit(dynamic_update_index_in_dim)/dynamic_update_slice | solution.py:94
  71.1 5.2 %fusion.237 = (bf16[1,128,64,256]{3,1,2,0:T(8,128)(2,1)}, bf16[1,128,64,256]{3,1,2,0:T(8,128)(2,1)S(1)}) fusion(bf16[2,128,64,256]{3,1,2,0:T(8,128)(2,1)} %get-tuple-element.40), kind=kLoop, calls=%fused_computation.416 | loop fusion | bytes 16777216 | tf_op jit(solution)/shard_map/slice | solution.py:15
  76.3 3.5 collective-permute-start.4
  81.1 87.4 %collective-permute-done.4 = bf16[1,128,64,256]{3,1,2,0:T(8,128)(2,1)S(1)} collective-permute-done((bf16[1,128,64,256]{3,1,2,0:T(8,128)(2,1)S(1)}, bf16[1,128,64,256]{3,1,2,0:T(8,128)(2,1)S(1)}, u32[]{:S(2)}, u32[]{:S(2)}) %collective-permute-start.4) | collective-permute-done | bytes 4194336 | tf_op jit(solution)/shard_map/ppermute | solution.py:19
  168.5 2.2 constant_dynamic-update-slice_fusion.57
  170.7 7.7 %constant_dynamic-update-slice_fusion.56 = bf16[4,128,64,256]{3,1,2,0:T(8,128)(2,1)} fusion(bf16[4,128,64,256]{3,1,2,0:T(8,128)(2,1)} %constant_dynamic-update-slice_fusion.57, bf16[2,128,64,256]{3,1,2,0:T(8,128)(2,1)} %get-tuple-element.40), kind=kLoop, calls=%fused_computation.205 | loop fusion | bytes 16777216
  178.5 2.2 constant_dynamic-update-slice_fusion.55
  183.7 2.4 collective-permute-start.7
  187.0 4.4 collective-permute-done.7
  191.4 5.9 %convolution_bitcast_fusion.2 = f32[36,2,66,256]{3,0,2,1:T(8,128)S(1)} fusion(bf16[108,128]{1,0:T(8,128)(2,1)S(1)} %copy-done.21, bf16[4,128,1,256]{3,1,2,0:T(8,128)(2,1)S(1)} %collective-permute-done.7, bf16[4,128,64,256]{3,1,2,0:T(8,128)(2,1)} %constant_dynamic-update-slice_fusion.55, bf16[4,128,1,256]{3,1,2,0:T(8,128)(2,1)S(1)} %collective-permute-done.6), kind=kOutput, calls=%fused_computation.13 | convolution fusion | flops 363331584 | bytes 22177792 | tf_op jit(solution)/shard_map/rh,zhyx->rzyx/dot_general | solution.py:100
  197.3 3.8 copy.225
  201.1 2.1 slice_bitcast_fusion.26
  207.4 6.0 %convolution_bitcast_fusion.1 = f32[36,2,66,256]{3,0,2,1:T(8,128)S(1)} fusion(bf16[108,128]{1,0:T(8,128)(2,1)S(1)} %copy-done.21, bf16[4,128,1,256]{3,1,2,0:T(8,128)(2,1)S(1)} %copy-done.18, bf16[4,128,64,256]{3,1,2,0:T(8,128)(2,1)} %constant_dynamic-update-slice_fusion.55, bf16[4,128,1,256]{3,1,2,0:T(8,128)(2,1)S(1)} %copy-done.15), kind=kOutput, calls=%fused_computation.12 | convolution fusion | flops 363331584 | bytes 22177792 | tf_op jit(solution)/shard_map/rh,zhyx->rzyx/dot_general | solution.py:100
  213.4 3.8 copy.226
  217.2 2.1 slice_bitcast_fusion.17
  223.6 6.2 %convolution_bitcast_fusion = f32[36,2,66,256]{3,0,2,1:T(8,128)} fusion(bf16[108,128]{1,0:T(8,128)(2,1)S(1)} %copy-done.21, bf16[4,128,1,256]{3,1,2,0:T(8,128)(2,1)S(1)} %copy-done.19, bf16[4,128,64,256]{3,1,2,0:T(8,128)(2,1)} %constant_dynamic-update-slice_fusion.55, bf16[4,128,1,256]{3,1,2,0:T(8,128)(2,1)S(1)} %copy-done.16), kind=kOutput, calls=%fused_computation.11 | convolution fusion | flops 363331584 | bytes 22177792 | tf_op jit(solution)/shard_map/rh,zhyx->rzyx/dot_general | solution.py:100
  229.8 6.3 %copy.227 = f32[36,2,66,256]{3,1,2,0:T(2,128)S(1)} copy(f32[36,2,66,256]{3,0,2,1:T(8,128)} %convolution_bitcast_fusion) | data formatting | bytes 9732096 | tf_op jit(solution)/shard_map/rh,zhyx->rzyx/dot_general | solution.py:100
  239.3 5.8 %fusion.38 = f32[4,2,64,256]{3,1,2,0:T(2,128)S(1)} fusion(f32[3,3,4,2,66,256]{5,3,4,2,1,0:T(2,128)S(1)} %bitcast.597, f32[3,3,4,2,66,256]{5,3,4,2,1,0:T(2,128)S(1)} %bitcast.595, f32[3,3,4,2,66,256]{5,3,4,2,1,0:T(2,128)S(1)} %bitcast.593, f32[4,2,64,255]{3,1,2,0:T(2,128)S(1)} %slice.681, f32[4,2,64,255]{3,1,2,0:T(2,128)S(1)} %bitcast.617, ...), kind=kLoop, calls=%fused_computation.67 | loop fusion | flops 3538944 | bytes 14643216 | tf_op jit(solution)/shard_map/add | solution.py:136
  246.3 8.7 %copy.228 = f32[4,2,64,256]{0,3,2,1:T(8,128)} copy(f32[4,2,64,256]{3,1,2,0:T(2,128)S(1)} %pad_maximum_fusion.3) | data formatting | bytes 1048576 | tf_op jit(solution)/shard_map/concatenate | solution.py:139
  255.0 13.4 %copy.230 = f32[2,2,2,4,1,32,128]{6,5,3,2,1,0,4:T(8,128)S(1)} copy(f32[2,2,2,4,1,32,128]{3,2,6,1,5,0,4:T(2,128)} %bitcast.588) | data formatting | bytes 1048576 | tf_op jit(solution)/shard_map/transpose | solution.py:143
  271.2 14.7 %all-to-all-start = ((f32[32,1,2048]{2,1,0:T(1,128)}), f32[32,1,2048]{2,1,0:T(1,128)S(1)}, u32[]{:S(2)}, u32[]{:S(2)}) async-start(f32[32,1,2048]{2,1,0:T(1,128)} %reshape.209), calls=%async_computation | async-start | bytes 524288 | tf_op jit(solution)/shard_map/all_to_all | solution.py:159
  286.1 9.5 %all-to-all-done = f32[32,1,2048]{2,1,0:T(1,128)S(1)} async-done(((f32[32,1,2048]{2,1,0:T(1,128)}), f32[32,1,2048]{2,1,0:T(1,128)S(1)}, u32[]{:S(2)}, u32[]{:S(2)}) %all-to-all-start) | async-done | bytes 262176 | tf_op jit(solution)/shard_map/all_to_all | solution.py:159
  303.6 3.4 all-to-all-start.1
  307.1 3.9 all-to-all-done.1
  316.7 1.9 fusion.6
  321.2 4.4 copy.247
  325.7 3.7 reshape.213
  329.4 11.6 %all_to_all.48 = f32[4,1,32768]{2,1,0:T(1,128)S(1)} all-to-all(f32[4,1,32768]{2,1,0:T(1,128)S(1)} %reshape.213), channel_id=1, replica_groups=mesh['gz'=32,'gy'=4] {'gy'}, dimensions={0} | all-to-all | bytes 1048576 | tf_op jit(solution)/shard_map/all_to_all | solution.py:199
  341.0 2.1 reduce.7
  343.1 3.4 reshape.214
  346.5 4.8 %copy.299 = f32[2,16,4,32,4,8]{3,2,5,4,1,0:T(4,128)S(1)} copy(f32[2,16,4,32,4,8]{1,5,4,0,3,2:T(8,128)} %bitcast.599) | data formatting | bytes 1048576 | tf_op jit(solution)/shard_map/all_to_all | solution.py:199
  357.6 2.2 reshape.215
  359.8 4.2 all-to-all-start.3
  364.1 11.6 %multiply_reduce_fusion = (f32[]{:T(128)}, f32[1,2,2,4,1,32,128]{3,2,6,1,5,0,4:T(2,128)}) fusion(f32[2,2,2,4,1,32,128]{3,2,6,1,5,0,4:T(2,128)} %bitcast.589), kind=kLoop, calls=%fused_computation.10 | loop fusion | flops 131071 | bytes 524292 | tf_op jit(solution)/shard_map/reduce_sum | solution.py:150
  387.4 7.7 %copy.229 = f32[1,2,2,4,1,32,128]{6,5,3,2,1,4,0:T(8,128)} copy(f32[1,2,2,4,1,32,128]{3,2,6,1,5,0,4:T(2,128)} %get-tuple-element.101) | data formatting | bytes 524288 | tf_op jit(solution)/shard_map/slice | solution.py:146
  395.2 66.3 %psum.34 = f32[]{:T(128)} all-reduce(f32[]{:T(128)S(6)} %add.357), channel_id=1, replica_groups=mesh['gz'=32,'gy'=4] {'gz','gy'}, use_global_device_ids=true, to_apply=%region_3.4 | all-reduce | flops 1 | bytes 8 | tf_op jit(solution)/shard_map/psum | solution.py:151
  (197 shorter events, 71.1 us)
Async XLA Ops:
  0.6 316.1 %copy-start = (f32[16,8,32]{2,1,0:T(8,128)S(1)}, f32[16,8,32]{2,1,0:T(8,128)}, u32[]{:S(2)}) copy-start(f32[16,8,32]{2,1,0:T(8,128)} %param.17) | copy-start | bytes 49156
  2.9 6.2 %collective-permute-start = (bf16[2,1,64,256]{3,1,2,0:T(2,128)(2,1)S(1)}, bf16[2,1,64,256]{3,1,2,0:T(2,128)(2,1)S(1)}, u32[]{:S(2)}, u32[]{:S(2)}) collective-permute-start(bf16[2,1,64,256]{3,1,2,0:T(2,128)(2,1)S(1)} %get-tuple-element.145), channel_id=1, source_target_pairs={{0,4},{4,8},{8,12},{12,16},{16,20},{20,24},{24,28},{28,32},{32,36}... | collective-permute-start | bytes 196616 | tf_op jit(solution)/shard_map/ppermute | solution.py:19
  6.9 5.7 %collective-permute-start.1 = (bf16[2,1,64,256]{3,1,2,0:T(2,128)(2,1)S(1)}, bf16[2,1,64,256]{3,1,2,0:T(2,128)(2,1)S(1)}, u32[]{:S(2)}, u32[]{:S(2)}) collective-permute-start(bf16[2,1,64,256]{3,1,2,0:T(2,128)(2,1)S(1)} %get-tuple-element.146), channel_id=1, source_target_pairs={{4,0},{8,4},{12,8},{16,12},{20,16},{24,20},{28,24},{32,28},{36,32}... | collective-permute-start | bytes 196616 | tf_op jit(solution)/shard_map/ppermute | solution.py:21
  12.6 7.5 %collective-permute-start.2 = (bf16[2,4,1,256]{3,1,2,0:T(4,128)(2,1)S(1)}, bf16[2,4,1,256]{3,1,2,0:T(4,128)(2,1)S(1)}, u32[]{:S(2)}, u32[]{:S(2)}) collective-permute-start(bf16[2,4,1,256]{3,1,2,0:T(4,128)(2,1)S(1)} %get-tuple-element.140), channel_id=1, source_target_pairs={{0,1},{1,2},{2,3},{4,5},{5,6},{6,7},{8,9},{9,10},{10,11},{12,13},{... | collective-permute-start | bytes 12296 | tf_op jit(solution)/shard_map/ppermute | solution.py:19
  18.2 4.9 %collective-permute-start.3 = (bf16[2,4,1,256]{3,1,2,0:T(4,128)(2,1)S(1)}, bf16[2,4,1,256]{3,1,2,0:T(4,128)(2,1)S(1)}, u32[]{:S(2)}, u32[]{:S(2)}) collective-permute-start(bf16[2,4,1,256]{3,1,2,0:T(4,128)(2,1)S(1)} %get-tuple-element.141), channel_id=1, source_target_pairs={{1,0},{2,1},{3,2},{5,4},{6,5},{7,6},{9,8},{10,9},{11,10},{13,12},{... | collective-permute-start | bytes 12296 | tf_op jit(solution)/shard_map/ppermute | solution.py:21
  31.8 2.5 copy-start.20
  31.9 2.5 copy-start.22
  31.9 2.5 copy-start.23
  31.9 2.5 copy-start.24
  76.3 92.2 %collective-permute-start.4 = (bf16[1,128,64,256]{3,1,2,0:T(8,128)(2,1)S(1)}, bf16[1,128,64,256]{3,1,2,0:T(8,128)(2,1)S(1)}, u32[]{:S(2)}, u32[]{:S(2)}) collective-permute-start(bf16[1,128,64,256]{3,1,2,0:T(8,128)(2,1)S(1)} %get-tuple-element.105), channel_id=1, source_target_pairs={{0,4},{4,8},{8,12},{12,16},{16,20},{20,24},{24,28},{28,32},{32,36}... | collective-permute-start | bytes 12582920 | tf_op jit(solution)/shard_map/ppermute | solution.py:19
  79.8 98.7 %collective-permute-start.5 = (bf16[1,128,64,256]{3,1,2,0:T(8,128)(2,1)}, bf16[1,128,64,256]{3,1,2,0:T(8,128)(2,1)S(1)}, u32[]{:S(2)}, u32[]{:S(2)}) collective-permute-start(bf16[1,128,64,256]{3,1,2,0:T(8,128)(2,1)} %get-tuple-element.104), channel_id=1, source_target_pairs={{4,0},{8,4},{12,8},{16,12},{20,16},{24,20},{28,24},{32,28},{36,32}... | collective-permute-start | bytes 12582920 | tf_op jit(solution)/shard_map/ppermute | solution.py:21
  178.4 12.9 %copy-start.21 = (bf16[108,128]{1,0:T(8,128)(2,1)S(1)}, bf16[108,128]{1,0:T(8,128)(2,1)}, u32[]{:S(2)}) copy-start(bf16[108,128]{1,0:T(8,128)(2,1)} %param.15) | copy-start | bytes 82948
  181.7 5.2 %collective-permute-start.6 = (bf16[4,128,1,256]{3,1,2,0:T(8,128)(2,1)S(1)}, bf16[4,128,1,256]{3,1,2,0:T(8,128)(2,1)S(1)}, u32[]{:S(2)}, u32[]{:S(2)}) collective-permute-start(bf16[4,128,1,256]{3,1,2,0:T(8,128)(2,1)S(1)} %get-tuple-element.102), channel_id=1, source_target_pairs={{0,1},{1,2},{2,3},{4,5},{5,6},{6,7},{8,9},{9,10},{10,11},{12,13},{... | collective-permute-start | bytes 786440 | tf_op jit(solution)/shard_map/ppermute | solution.py:19
  183.7 7.7 %collective-permute-start.7 = (bf16[4,128,1,256]{3,1,2,0:T(8,128)(2,1)S(1)}, bf16[4,128,1,256]{3,1,2,0:T(8,128)(2,1)S(1)}, u32[]{:S(2)}, u32[]{:S(2)}) collective-permute-start(bf16[4,128,1,256]{3,1,2,0:T(8,128)(2,1)S(1)} %get-tuple-element.103), channel_id=1, source_target_pairs={{1,0},{2,1},{3,2},{5,4},{6,5},{7,6},{9,8},{10,9},{11,10},{13,12},{... | collective-permute-start | bytes 786440 | tf_op jit(solution)/shard_map/ppermute | solution.py:21
  187.0 10.3 %copy-start.14 = (bf16[4,128,1,256]{3,1,2,0:T(8,128)(2,1)}, bf16[4,128,1,256]{3,1,2,0:T(8,128)(2,1)S(1)}, u32[]{:S(2)}) copy-start(bf16[4,128,1,256]{3,1,2,0:T(8,128)(2,1)S(1)} %collective-permute-done.6) | copy-start | bytes 786436
  191.4 5.9 %copy-start.17 = (bf16[4,128,1,256]{3,1,2,0:T(8,128)(2,1)}, bf16[4,128,1,256]{3,1,2,0:T(8,128)(2,1)S(1)}, u32[]{:S(2)}) copy-start(bf16[4,128,1,256]{3,1,2,0:T(8,128)(2,1)S(1)} %collective-permute-done.7) | copy-start | bytes 786436
  201.1 6.4 %copy-start.15 = (bf16[4,128,1,256]{3,1,2,0:T(8,128)(2,1)S(1)}, bf16[4,128,1,256]{3,1,2,0:T(8,128)(2,1)}, u32[]{:S(2)}) copy-start(bf16[4,128,1,256]{3,1,2,0:T(8,128)(2,1)} %copy-done.14) | copy-start | bytes 786436
  201.1 6.3 %copy-start.18 = (bf16[4,128,1,256]{3,1,2,0:T(8,128)(2,1)S(1)}, bf16[4,128,1,256]{3,1,2,0:T(8,128)(2,1)}, u32[]{:S(2)}) copy-start(bf16[4,128,1,256]{3,1,2,0:T(8,128)(2,1)} %copy-done.17) | copy-start | bytes 786436
  217.2 6.4 %copy-start.16 = (bf16[4,128,1,256]{3,1,2,0:T(8,128)(2,1)S(1)}, bf16[4,128,1,256]{3,1,2,0:T(8,128)(2,1)}, u32[]{:S(2)}) copy-start(bf16[4,128,1,256]{3,1,2,0:T(8,128)(2,1)} %copy-done.14) | copy-start | bytes 786436
  217.2 6.4 %copy-start.19 = (bf16[4,128,1,256]{3,1,2,0:T(8,128)(2,1)S(1)}, bf16[4,128,1,256]{3,1,2,0:T(8,128)(2,1)}, u32[]{:S(2)}) copy-start(bf16[4,128,1,256]{3,1,2,0:T(8,128)(2,1)} %copy-done.17) | copy-start | bytes 786436
  236.1 3.0 copy-start.1
  236.1 3.0 copy-start.2
  236.1 3.0 copy-start.3
  236.1 3.0 copy-start.4
  236.1 3.0 copy-start.5
  236.2 3.0 copy-start.6
  236.2 3.0 copy-start.7
  236.2 3.0 copy-start.8
  236.2 3.0 copy-start.9
  236.2 3.0 copy-start.10
  236.2 3.0 copy-start.11
  236.2 3.0 copy-start.13
  239.3 5.9 %copy-start.12 = (f32[2,2,64,256]{3,2,1,0:T(8,128)S(1)}, f32[2,2,64,256]{3,2,1,0:T(8,128)}, u32[]{:S(2)}) copy-start(f32[2,2,64,256]{3,2,1,0:T(8,128)} %get-tuple-element.136) | copy-start | bytes 786436
  271.2 24.3 %all-to-all-start = ((f32[32,1,2048]{2,1,0:T(1,128)}), f32[32,1,2048]{2,1,0:T(1,128)S(1)}, u32[]{:S(2)}, u32[]{:S(2)}) async-start(f32[32,1,2048]{2,1,0:T(1,128)} %reshape.209), calls=%async_computation | async-start | bytes 524288 | tf_op jit(solution)/shard_map/all_to_all | solution.py:159
  303.6 7.4 %all-to-all-start.1 = ((f32[4,1,16384]{2,1,0:T(1,128)}), f32[4,1,16384]{2,1,0:T(1,128)S(1)}, u32[]{:S(2)}, u32[]{:S(2)}) async-start(f32[4,1,16384]{2,1,0:T(1,128)} %reshape.211), calls=%async_computation.1 | async-start | bytes 524288 | tf_op jit(solution)/shard_map/all_to_all | solution.py:168
  359.8 17.2 %all-to-all-start.3 = ((f32[32,1,4096]{2,1,0:T(1,128)}), f32[32,1,4096]{2,1,0:T(1,128)S(1)}, u32[]{:S(2)}, u32[]{:S(2)}) async-start(f32[32,1,4096]{2,1,0:T(1,128)} %reshape.215), calls=%async_computation.3 | async-start | bytes 1048576 | tf_op jit(solution)/shard_map/all_to_all | solution.py:208
where the time goes:
time: 472 us; the launch traced here: 463 us
  local copies, waits for them, and re-layouts  146 us (31%)
  waiting for transfers between devices  113 us (24%)
  blocking collectives  77.9 us (17%)
  matrix products  45.1 us (10%)
  starting transfers between devices  44.3 us (9%)
  other arithmetic  30.7 us (7%)
  between operations  6.17 us (1%)
    ppermute x4, waiting for transfers between devices, with_halo(): lax.ppermute(tail, axis, [(i, (i + 1) % count) for i in range(ends)])  88.9 us
    psum x1, blocking collectives, shards(): early_totals = lax.psum((first_term, split_term), ('gz', 'gy'))  66.3 us
    unnamed x113, local copies, waits for them, and re-layouts  30.2 us
    dynamic_update_slice x4, local copies, waits for them, and re-layouts, hidden_layers(): return lax.map(one_plane, columns)  22 us
    dot_general x3, matrix products, conv_wide(): jnp.einsum('rh,zhyx->rzyx', output_weight[36 * z_tap:36 * (z_tap + 1)], w...  18.1 us
    ppermute x4, starting transfers between devices, with_halo(): lax.ppermute(tail, axis, [(i, (i + 1) % count) for i in range(ends)])  14.9 us
    all_to_all x1, starting transfers between devices, shards(): lax.all_to_all(jnp.stack([real_x, imag_x]), 'gz', split_axis=4, concat_ax...  14.7 us
    dot_general x3, local copies, waits for them, and re-layouts, conv_wide(): jnp.einsum('rh,zhyx->rzyx', output_weight[36 * z_tap:36 * (z_tap + 1)], w...  13.8 us
  transfers between devices with their start and end apart: 11, of which 8 were waited for; matrix products, arithmetic and copies ran while one was open for 5% of the time, Pallas kernels for 0%

commit v1 on v0

v1 whole, which is shorter than its diff:
```python
import functools
import math

import jax
import jax.numpy as jnp
import ml_dtypes
import numpy as np
from jax import lax
from jax.experimental import pallas as pl
from jax.experimental.pallas import tpu as pltpu
from jax.sharding import PartitionSpec as P

MESH = pl.DeviceIdType.MESH
F32 = jnp.float32
BF16 = jnp.bfloat16

SLOTS = 40
ROWS = 64
WIDE = 256
GZ = 32
GY = 4
OWN_ROWS = ROWS + 2


def real_basis(length):
    cells = np.arange(length)
    rows = [np.full(length, 1.0 / math.sqrt(length))]
    for m in range(1, length // 2):
        rows.append(math.sqrt(2.0 / length) * np.cos(2.0 * math.pi * m * cells / length))
        rows.append(math.sqrt(2.0 / length) * np.sin(2.0 * math.pi * m * cells / length))
    rows.append(np.where(cells % 2 == 0, 1.0, -1.0) / math.sqrt(length))
    return np.stack(rows)


def split_pair(table):
    table = np.asarray(table, np.float32)
    high = table.astype(ml_dtypes.bfloat16)
    low = (table - high.astype(np.float32)).astype(ml_dtypes.bfloat16)
    return np.stack([high, low])


def tables():
    fx, fy, fz = real_basis(128), real_basis(128), real_basis(32)
    forward_x = np.zeros((128, 2, 128, 2))
    for k in range(2):
        forward_x[:, k, :, k] = fx
    forward_x = forward_x.reshape(256, 256)
    forward_z = np.einsum("kz,qp->qkzp", fz, np.eye(8)).reshape(256, 256)
    forward_y = np.einsum("kgy,cd->gcydk", fy.reshape(128, 4, 32), np.eye(4)).reshape(512, 512)
    spread = np.zeros((128, 2, 2, 128))
    for k in range(2):
        spread[np.arange(128), k, k, np.arange(128)] = 1.0
    spread = spread.reshape(256, 256).astype(ml_dtypes.bfloat16)
    pick = np.zeros((64, 4, 128))
    for plane in range(4):
        for c in range(2):
            for a in range(3):
                for b in range(3):
                    for e in range(3):
                        row = 27 * c + 9 * a + 3 * b + e
                        pick[row, plane, b * SLOTS + e * 12 + (a + plane) * 2 + c] = 1.0
        for piece in range(3):
            pick[54 + piece, plane, piece * SLOTS + 36] = 1.0
    pick = pick.reshape(64, 512).astype(ml_dtypes.bfloat16)
    half_z = (np.arange(32) + 1) // 2 / 32.0
    half_y = (np.arange(128) + 1) // 2 / 128.0
    squares = (half_z[:, None] ** 2 + half_y[None, :] ** 2).reshape(1, 4096).astype(np.float32)
    return {
        "forward_x": split_pair(forward_x),
        "forward_z": split_pair(forward_z),
        "backward_z": split_pair(forward_z.T),
        "forward_y": split_pair(forward_y),
        "backward_x": split_pair(fx.T),
        "spread": spread,
        "pick": pick,
        "squares": squares,
    }


def split2(values):
    high = values.astype(BF16)
    return high, (values - high.astype(F32)).astype(BF16)


def split3(values):
    high = values.astype(BF16)
    rest = values - high.astype(F32)
    mid = rest.astype(BF16)
    return high, mid, (rest - mid.astype(F32)).astype(BF16)


def mul(a, b, dims=((1,), (0,))):
    return lax.dot_general(a, b, (dims, ((), ())), preferred_element_type=F32)


def mul3(a, b, dims=((1,), (0,))):
    return mul(a[0], b[0], dims) + (mul(a[0], b[1], dims) + mul(a[1], b[0], dims))


def shift_right(values):
    lane = lax.broadcasted_iota(jnp.int32, values.shape, values.ndim - 1)
    return jnp.where(lane == 0, 0.0, pltpu.roll(values, 1, values.ndim - 1))


def shift_left(values):
    last = values.shape[-1] - 1
    lane = lax.broadcasted_iota(jnp.int32, values.shape, values.ndim - 1)
    return jnp.where(lane == last, 0.0, pltpu.roll(values, last, values.ndim - 1))


def flow_kernel(
    dens, first_w, first_b, middle_w, middle_b, output_w, output_b, radial,
    forward_x, forward_z, backward_z, forward_y, backward_x, spread, pick, squares,
    factored, latent, log_density,
    lower_send, edge_send, lower_prev, lower_next, edge_recv,
    window, hidden, acc0, acc1, wide_w, w1, w2, b2, w3, ow32, profile,
    x_send, z_recv, z_send, y_recv, mixed, y_send, yb_recv, zb_send, x_recv, flat,
    kept, sum_send, sum_gz, sum_gy, dens2,
    halo_ssem, halo_rsem, gz_ssem, gz_rsem, gy_ssem, gy_rsem,
):
    me_z = lax.axis_index("gz")
    me_y = lax.axis_index("gy")

    def near_z(step):
        return lax.rem(me_z + step + GZ, GZ)

    def near_y(step):
        return lax.rem(me_y + step + GY, GY)

    barrier = pltpu.get_barrier_semaphore()

    def greet_z(i, carry):
        pl.semaphore_signal(barrier, inc=1, device_id=(near_z(i), me_y), device_id_type=MESH)
        return carry

    lax.fori_loop(1, GZ, greet_z, 0)
    for i in range(1, GY):
        pl.semaphore_signal(barrier, inc=1, device_id=(me_z, near_y(i)), device_id_type=MESH)
    for dz in (-1, 1):
        for dy in (-1, 1):
            pl.semaphore_signal(
                barrier, inc=1, device_id=(near_z(dz), near_y(dy)), device_id_type=MESH
            )

    for z in range(2):
        for c in range(2):
            lower_send[z, c] = dens[c, z].astype(BF16)
    for side in range(2):
        for row in range(2):
            for z in range(2):
                for c in range(2):
                    source_row = row if side == 0 else ROWS - 2 + row
                    line = dens[c, z, pl.ds(source_row, 1), :]
                    edge_send[side, pl.ds(row * 4 + z * 2 + c, 1), :] = line.astype(BF16).astype(F32)

    pl.semaphore_wait(barrier, (GZ - 1) + (GY - 1) + 4)

    halo = []

    def send_halo(src, dst, index, to):
        copy = pltpu.make_async_remote_copy(
            src_ref=src, dst_ref=dst, send_sem=halo_ssem.at[index], recv_sem=halo_rsem.at[index],
            device_id=to, device_id_type=MESH,
        )
        copy.start()
        halo.append(copy)

    send_halo(lower_send.at[1], lower_prev.at[1], 0, (near_z(1), me_y))
    send_halo(lower_send.at[0], lower_next.at[0], 1, (near_z(-1), me_y))
    send_halo(lower_send.at[1], lower_next.at[1], 2, (near_z(-1), me_y))
    send_halo(lower_send.at[0], lower_prev.at[0], 3, (near_z(1), me_y))
    index = 4
    for side in range(2):
        to_y = near_y(-1) if side == 0 else near_y(1)
        for dz in (-1, 0, 1):
            send_halo(
                edge_send.at[side], edge_recv.at[1 - side, 1 - dz], index, (near_z(dz), to_y)
            )
            index += 1

    for half in range(2):
        dens2[half] = dens[:, :, :, pl.ds(half * 128, 128)]

    wide_w[...] = jnp.zeros_like(wide_w)
    wide_w[pl.ds(0, 54), :] = first_w[...].astype(F32)
    for piece, part in enumerate(split3(first_b[...])):
        wide_w[pl.ds(54 + piece, 1), :] = part.astype(F32)
    turned = jnp.transpose(wide_w[...]).astype(BF16)
    for plane in range(4):
        w1[pl.ds(plane * 128, 128), :] = mul(
            turned, pick[:, pl.ds(plane * 128, 128)]
        ).astype(BF16)
    w2[...] = jnp.transpose(middle_w[...].astype(F32)).astype(BF16)
    b2[...] = jnp.transpose(jnp.broadcast_to(middle_b[...], (128, 128)))
    ow32[...] = output_w[...].astype(F32)
    w3[...] = jnp.zeros_like(w3)
    for a in range(3):
        for b in range(3):
            w3[pl.ds(b * 16, 12), pl.ds(a * 128, 128)] = ow32[pl.ds(36 * a + 12 * b, 12), :]

    step_x = (me_z * 4 + me_y + 1) // 2
    freq_x = step_x.astype(F32) * (1.0 / 128.0)
    weights = radial[...]
    centres = lax.broadcasted_iota(jnp.int32, (32, 512), 0).astype(F32)

    def filter_part(part, carry):
        lanes = pl.ds(pl.multiple_of(part * 512, 512), 512)
        kappa = jnp.sqrt(squares[:, lanes] + freq_x * freq_x) * (2.0 / math.sqrt(3.0))
        scaled = kappa * 31.0 - centres
        basis = jnp.exp(-scaled * scaled)
        values = mul3(split2(weights), split2(basis))
        for j in range(4):
            profile[pl.ds(part * 4 + j, 128, stride=32), :] = values[:, j * 128 : (j + 1) * 128]
        return carry

    lax.fori_loop(0, 8, filter_part, 0)

    def put(first, count, slot, values):
        for e, shifted in enumerate((shift_right(values), values, shift_left(values))):
            for half in range(2):
                window[half, pl.ds(first * SLOTS + e * 12 + slot, count, stride=SLOTS), :] = shifted[
                    :, half * 128 : (half + 1) * 128
                ]

    for half in range(2):
        window[half, pl.ds(36, 72, stride=SLOTS), :] = jnp.ones((72, 128), F32)
        for slot in range(37, 40):
            window[half, pl.ds(slot, 72, stride=SLOTS), :] = jnp.zeros((72, 128), F32)
        window[half, pl.ds(68 * SLOTS, 36), :] = jnp.zeros((36, 128), F32)
    for z in range(2):
        for c in range(2):
            put(2, ROWS, (z + 2) * 2 + c, dens[c, z].astype(BF16).astype(F32))

    for copy in halo:
        copy.wait()

    has_prev = me_z > 0
    has_next = me_z < GZ - 1
    has_up = me_y > 0
    has_down = me_y < GY - 1
    for z in range(2):
        for c in range(2):
            put(2, ROWS, z * 2 + c, jnp.where(has_prev, lower_prev[z, c].astype(F32), 0.0))
            put(2, ROWS, (z + 4) * 2 + c, jnp.where(has_next, lower_next[z, c].astype(F32), 0.0))
    for side in range(2):
        for offset in range(3):
            valid = has_up if side == 0 else has_down
            if offset == 0:
                valid = jnp.logical_and(valid, has_prev)
            if offset == 2:
                valid = jnp.logical_and(valid, has_next)
            for row in range(2):
                lines = edge_recv[side, offset, pl.ds(row * 4, 4), :]
                lines = jnp.where(valid, lines, 0.0)
                at = (row if side == 0 else ROWS + 2 + row) * SLOTS + offset * 4
                for e, shifted in enumerate((shift_right(lines), lines, shift_left(lines))):
                    for half in range(2):
                        window[half, pl.ds(at + e * 12, 4), :] = shifted[
                            :, half * 128 : (half + 1) * 128
                        ]

    w3_lane = lax.broadcasted_iota(jnp.int32, (48, 384), 1)
    w3_first = jnp.where(jnp.logical_and(w3_lane < 128, me_z == 0), 0.0, w3[...]).astype(BF16)
    w3_second = jnp.where(
        jnp.logical_and(w3_lane >= 256, me_z == GZ - 1), 0.0, w3[...]
    ).astype(BF16)

    def columns(r):
        start = pl.multiple_of((r - 1) * SLOTS, 8)
        return jnp.concatenate(
            [window[0, pl.ds(start, 128), :], window[1, pl.ds(start, 128), :]], axis=1
        ).astype(BF16)

    def second(first_layer):
        values = mul(w2[...], first_layer) + jnp.concatenate([b2[...]] * 2, axis=1)
        return jnp.maximum(values, 0.0).astype(BF16)

    def add_taps(acc, r, taps):
        valid = jnp.logical_not(
            jnp.logical_or(
                jnp.logical_and(r == 1, me_y == 0),
                jnp.logical_and(r == OWN_ROWS, me_y == GY - 1),
            )
        )
        taps = jnp.where(valid, taps, 0.0)
        for half in range(2):
            part = taps[:, half * 128 : (half + 1) * 128]
            at = [pl.ds(pl.multiple_of((r + 1 - b) * 16, 16), 16) for b in range(3)]
            acc[half, at[0], :] = part[0:16]
            acc[half, at[1], :] += part[16:32]
            acc[half, at[2], :] += part[32:48]

    for acc in (acc0, acc1):
        for half in range(2):
            acc[half, pl.ds(0, 32), :] = jnp.zeros((32, 128), F32)

    def later_planes(pair, carry):
        for sub in range(2):
            r = pair * 2 + 1 + sub
            first_layer = jnp.maximum(mul(w1[pl.ds(128, 384), :], columns(r)), 0.0).astype(BF16)
            layers = [second(first_layer[p * 128 : (p + 1) * 128]) for p in range(3)]
            stacked = jnp.concatenate(layers, axis=0)
            hidden[r] = stacked[0:256]
            add_taps(acc1, r, mul(w3_second, stacked))
        return carry

    def first_plane(pair, carry):
        for sub in range(2):
            r = pair * 2 + 1 + sub
            first_layer = jnp.maximum(mul(w1[pl.ds(0, 128), :], columns(r)), 0.0).astype(BF16)
            stacked = jnp.concatenate([second(first_layer), hidden[r]], axis=0)
            add_taps(acc0, r, mul(w3_first, stacked))
        return carry

    lax.fori_loop(0, OWN_ROWS // 2, later_planes, 0)

    def couple(acc, z, parity):
        raw = []
        for o in range(4):
            taps = [
                jnp.concatenate(
                    [
                        acc[half, pl.ds((2 + parity) * 16 + e * 4 + o, 32, stride=32), :]
                        for half in range(2)
                    ],
                    axis=1,
                )
                for e in range(3)
            ]
            raw.append(shift_right(taps[0]) + taps[1] + shift_left(taps[2]) + output_b[o])
        lines = [
            jnp.concatenate(
                [
                    dens2[half, c, z, pl.ds(parity, 32, stride=2), :]
                    for half in range(2)
                ],
                axis=1,
            )
            for c in range(4)
        ]
        scales = [jnp.tanh(raw[0]), jnp.tanh(raw[1])]
        for o in range(2):
            lines[2 + o] = lines[2 + o] * jnp.exp(scales[o]) + raw[2 + o]
        return jnp.concatenate(lines, axis=0), scales[0] + scales[1]

    def spread_x(values):
        high, mid, low = split3(values)
        return mul(high, spread[...]) + (mul(mid, spread[...]) + mul(low, spread[...]))

    def fold(values):
        rows, lanes = values.shape
        total = values[:, 0:128]
        for at in range(128, lanes, 128):
            total = total + values[:, at : at + 128]
        return jnp.sum(total.reshape(rows // 8, 8, 128), axis=0)

    source, scale_sum = couple(acc1, 1, 0)
    kept[0] = source
    total = fold(scale_sum)
    x_modes = mul3(
        (forward_x[0], forward_x[1]), split2(source), ((1,), (1,))
    )
    x_send[...] = x_modes.reshape(GZ, 8, 128)

    def send_all_gz(src, dst, stage):
        def one(i, carry):
            to = near_z(i)
            pltpu.make_async_remote_copy(
                src_ref=src.at[to], dst_ref=dst.at[me_z], send_sem=gz_ssem.at[stage], recv_sem=gz_rsem.at[stage],
                device_id=(to, me_y), device_id_type=MESH,
            ).start()
            return carry

        lax.fori_loop(1, GZ, one, 0)
        dst[me_z] = src[me_z]

    def wait_all_gz(src, dst, stage):
        copy = pltpu.make_async_remote_copy(
            src_ref=src.at[pl.ds(0, GZ - 1)], dst_ref=dst.at[pl.ds(0, GZ - 1)],
            send_sem=gz_ssem.at[stage], recv_sem=gz_rsem.at[stage],
            device_id=(near_z(1), me_y), device_id_type=MESH,
        )
        copy.wait()

    def send_all_gy(src, dst, stage):
        for i in range(1, GY):
            to = near_y(i)
            pltpu.make_async_remote_copy(
                src_ref=src.at[to], dst_ref=dst.at[me_y], send_sem=gy_ssem.at[stage], recv_sem=gy_rsem.at[stage],
                device_id=(me_z, to), device_id_type=MESH,
            ).start()
        dst[me_y] = src[me_y]

    def wait_all_gy(src, dst, stage):
        copy = pltpu.make_async_remote_copy(
            src_ref=src.at[pl.ds(0, GY - 1)], dst_ref=dst.at[pl.ds(0, GY - 1)],
            send_sem=gy_ssem.at[stage], recv_sem=gy_rsem.at[stage],
            device_id=(me_z, near_y(1)), device_id_type=MESH,
        )
        copy.wait()

    send_all_gz(x_send, z_recv, 0)
    kept[1], scale_sum = couple(acc1, 1, 1)
    total = total + fold(scale_sum)
    lax.fori_loop(0, 8, first_plane, 0)
    wait_all_gz(x_send, z_recv, 0)

    z_modes = mul3((forward_z[0], forward_z[1]), split2(z_recv[...].reshape(256, 128)))
    z_send[...] = z_modes.reshape(GY, 64, 128)
    send_all_gy(z_send, y_recv, 0)
    lax.fori_loop(8, 16, first_plane, 0)
    wait_all_gy(z_send, y_recv, 0)

    lines = jnp.concatenate([y_recv[g] for g in range(GY)], axis=1)
    modes = mul3(split2(lines), (forward_y[0], forward_y[1]))
    parts = [
        modes[k * 32 : (k + 1) * 32, c * 128 : (c + 1) * 128] for k in range(2) for c in range(4)
    ]
    for o in range(16):
        value = profile[pl.ds(o * 256, 32), :] * parts[0]
        for c in range(1, 8):
            value = value + profile[pl.ds(o * 256 + c * 32, 32), :] * parts[c]
        mixed[pl.ds((o // 4) * 32, 32), pl.ds((o % 4) * 128, 128)] = value
    back = mul3(split2(mixed[...]), (forward_y[0], forward_y[1]), ((1,), (1,)))
    for g in range(GY):
        y_send[g] = back[:, g * 128 : (g + 1) * 128]
    send_all_gy(y_send, yb_recv, 1)
    lax.fori_loop(16, 24, first_plane, 0)
    wait_all_gy(y_send, yb_recv, 1)

    for pair in range(2):
        lines = yb_recv[pl.ds(pair * 2, 2)].reshape(256, 128)
        planes = mul3((backward_z[0], backward_z[1]), split2(lines))
        zb_send[:, pl.ds(pair * 8, 8), :] = planes.reshape(GZ, 8, 128)
    send_all_gz(zb_send, x_recv, 1)

    lax.fori_loop(24, OWN_ROWS // 2, first_plane, 0)
    squares_sum = jnp.zeros((8, 128), F32)
    for parity in range(2):
        coupled, scale_sum = couple(acc0, 0, parity)
        total = total + fold(scale_sum)
        squares_sum = squares_sum + fold(coupled * coupled)
        coupled = spread_x(coupled)
        for k in range(2):
            at = (2 * parity + k) * 4
            factored[pl.ds(at, 4), 0] = coupled[:, k * 128 : (k + 1) * 128].reshape(4, 32, 128)
    source = spread_x(kept[0])
    squares_sum = squares_sum + fold(source * source)
    for k in range(2):
        latent[pl.ds(k * 4, 4), 0] = source[:, k * 128 : (k + 1) * 128].reshape(4, 32, 128)
    target = spread_x(kept[1])
    wait_all_gz(zb_send, x_recv, 1)

    flat[...] = x_recv[...].reshape(512, 128)
    shifts = []
    for og in range(4):
        lines = flat[pl.ds(og, 128, stride=4), :]
        shifts.append(jnp.transpose(mul3((backward_x[0], backward_x[1]), split2(lines))))
    for k in range(2):
        scale = jnp.tanh(shifts[k])
        total = total + fold(scale)
        moved = target[:, k * 128 : (k + 1) * 128] * jnp.exp(scale) + shifts[2 + k]
        squares_sum = squares_sum + fold(moved * moved)
        latent[pl.ds(8 + k * 4, 4), 0] = moved.reshape(4, 32, 128)

    total = total - 0.5 * squares_sum
    sum_send[...] = jnp.broadcast_to(total[None], sum_send.shape)
    send_all_gz(sum_send, sum_gz, 2)
    wait_all_gz(sum_send, sum_gz, 2)
    total = jnp.sum(sum_gz[...], axis=0)
    sum_send[pl.ds(0, GY)] = jnp.broadcast_to(total[None], (GY, 8, 128))
    send_all_gy(sum_send, sum_gy, 2)
    wait_all_gy(sum_send, sum_gy, 2)
    total = jnp.sum(sum_gy[...], axis=0)
    count = 4.0 * 64 * 256 * 256
    log_density[0, 0] = jnp.sum(total) / count - 0.5 * math.log(2.0 * math.pi)


def shards(consts, density_field, first_weight, first_bias, middle_weight, middle_bias, output_weight, output_bias, radial_weights):
    vmem = pl.BlockSpec(memory_space=pltpu.VMEM)
    smem = pl.BlockSpec(memory_space=pltpu.SMEM)
    operands = [
        density_field, first_weight, first_bias.reshape(1, 128), middle_weight,
        middle_bias.reshape(1, 128), output_weight, output_bias, radial_weights.reshape(128, 32),
    ] + [jnp.asarray(value) for value in consts.values()]
    specs = [vmem] * len(operands)
    specs[6] = smem
    buffers = [
        pltpu.VMEM((2, 2, ROWS, WIDE), BF16),
        pltpu.VMEM((2, 8, WIDE), F32),
        pltpu.VMEM((2, 2, ROWS, WIDE), BF16),
        pltpu.VMEM((2, 2, ROWS, WIDE), BF16),
        pltpu.VMEM((2, 3, 8, WIDE), F32),
        pltpu.VMEM((2, 72 * SLOTS, 128), F32),
        pltpu.VMEM((OWN_ROWS + 2, 256, WIDE), BF16),
        pltpu.VMEM((2, 70 * 16, 128), F32),
        pltpu.VMEM((2, 70 * 16, 128), F32),
        pltpu.VMEM((64, 128), F32),
        pltpu.VMEM((512, 128), BF16),
        pltpu.VMEM((128, 128), BF16),
        pltpu.VMEM((128, 128), F32),
        pltpu.VMEM((48, 384), F32),
        pltpu.VMEM((108, 128), F32),
        pltpu.VMEM((128 * 32, 128), F32),
        pltpu.VMEM((GZ, 8, 128), F32),
        pltpu.VMEM((GZ, 8, 128), F32),
        pltpu.VMEM((GY, 64, 128), F32),
        pltpu.VMEM((GY, 64, 128), F32),
        pltpu.VMEM((128, 512), F32),
        pltpu.VMEM((GY, 128, 128), F32),
        pltpu.VMEM((GY, 128, 128), F32),
        pltpu.VMEM((GZ, 16, 128), F32),
        pltpu.VMEM((GZ, 16, 128), F32),
        pltpu.VMEM((512, 128), F32),
        pltpu.VMEM((2, 128, WIDE), F32),
        pltpu.VMEM((GZ, 8, 128), F32),
        pltpu.VMEM((GZ, 8, 128), F32),
        pltpu.VMEM((GY, 8, 128), F32),
        pltpu.VMEM((2, 4, 2, ROWS, 128), F32),
        pltpu.SemaphoreType.DMA((10,)),
        pltpu.SemaphoreType.DMA((10,)),
        pltpu.SemaphoreType.DMA((3,)),
        pltpu.SemaphoreType.DMA((3,)),
        pltpu.SemaphoreType.DMA((3,)),
        pltpu.SemaphoreType.DMA((3,)),
    ]
    factored, latent, log_density = pl.pallas_call(
        flow_kernel,
        out_shape=(
            jax.ShapeDtypeStruct((16, 1, 32, 128), F32),
            jax.ShapeDtypeStruct((16, 1, 32, 128), F32),
            jax.ShapeDtypeStruct((1, 1), F32),
        ),
        in_specs=specs,
        out_specs=(vmem, vmem, smem),
        scratch_shapes=buffers,
        compiler_params=pltpu.CompilerParams(
            collective_id=0, has_side_effects=True, vmem_limit_bytes=48 * 1024 * 1024
        ),
        name="flow",
    )(*operands)
    return factored, latent, log_density.reshape(())


def solution(mesh):
    assert mesh.shape["gz"] == GZ and mesh.shape["gy"] == GY
    in_specs = (P(None, "gz", "gy", None), P(), P(), P(), P(), P(), P(), P())
    out_specs = (P(None, "gz", "gy", None), P(None, "gz", "gy", None), P())
    return jax.shard_map(
        functools.partial(shards, tables()),
        mesh=mesh, in_specs=in_specs, out_specs=out_specs, check_vma=False,
    )
```

time: 472 us -> 96.9 us (0.21); the launches traced: 463 us -> 96.2 us
  local copies, waits for them, and re-layouts: 146 us -> 12.8 us
  waiting for transfers between devices: 113 us -> 0 us
  Pallas kernels: 0 us -> 80.9 us
  blocking collectives: 77.9 us -> 0 us
  matrix products: 45.1 us -> 0 us
  starting transfers between devices: 44.3 us -> 0 us
  other arithmetic: 30.7 us -> 0 us
    ppermute x8 -> x0, waiting for transfers between devices: 99.8 us -> none  [the longest x4 88.9 us: with_halo(): lax.ppermute(tail, axis, [(i, (i + 1) % count) for i in range(ends)])]
    pallas_call x0 -> x1, Pallas kernels: none -> 80.9 us  [shards(): pl.pallas_call(flow_kernel, out_shape=(jax.ShapeDtypeStruct((16, 1, 32, 1...]
    psum x1 -> x0, blocking collectives: 66.3 us -> none  [shards(): early_totals = lax.psum((first_term, split_term), ('gz', 'gy'))]
    dot_general x26 -> x0, matrix products: 45.1 us -> none  [the longest x3 18.1 us: conv_wide(): jnp.einsum('rh,zhyx->rzyx', output_weight[36 * z_tap:36 * (z_tap + 1)], w...]
    slice x22 -> x0, local copies, waits for them, and re-layouts: 27.3 us -> none  [the longest x9 10.3 us: take_offset(): lax.slice_in_dim(values, 1, length, axis=along_axis)]
    all_to_all x3 -> x0, starting transfers between devices: 22.4 us -> none  [the longest x1 14.7 us: shards(): lax.all_to_all(jnp.stack([real_x, imag_x]), 'gz', split_axis=4, concat_ax...]
    dynamic_update_slice x4 -> x0, local copies, waits for them, and re-layouts: 22 us -> none  [hidden_layers(): return lax.map(one_plane, columns)]
    ppermute x8 -> x0, starting transfers between devices: 21.9 us -> none  [the longest x4 14.9 us: with_halo(): lax.ppermute(tail, axis, [(i, (i + 1) % count) for i in range(ends)])]
  transfers between devices with their start and end apart: 11 -> 0, of which waited for: 8 -> 0; matrix products, arithmetic and copies ran while one was open for 5% -> 0% of each run, Pallas kernels for 0% -> 0%
where the time goes in v1:
time: 96.9 us; the launch traced here: 96.2 us
  Pallas kernels  80.9 us (83%)
  local copies, waits for them, and re-layouts  12.8 us (13%)
  between operations  2.46 us (3%)
    pallas_call x1, Pallas kernels, shards(): pl.pallas_call(flow_kernel, out_shape=(jax.ShapeDtypeStruct((16, 1, 32, 1...  80.9 us
    unnamed x34, local copies, waits for them, and re-layouts  12.8 us

profile of v1, /device:TPU:1, one launch (start us, length us, event | category | flops | bytes accessed | tf_op | source)
XLA Modules:
  0.0 96.2 jit_solution(14397168677107247468)
XLA Ops:
  0.6 0.0 copy-start.11
  0.6 0.0 copy-start.13
  0.7 0.0 copy-start.14
  0.7 0.0 copy-start.15
  0.7 0.7 copy-done.11
  1.4 0.0 copy-done.13
  1.4 0.0 copy-done.14
  1.4 0.0 copy-done.15
  1.4 0.0 copy-start
  1.4 1.2 %copy-done = bf16[2,512,512]{2,1,0:T(8,128)(2,1)S(1)} copy-done((bf16[2,512,512]{2,1,0:T(8,128)(2,1)S(1)}, bf16[2,512,512]{2,1,0:T(8,128)(2,1)}, u32[]{:S(2)}) %copy-start) | copy-done | bytes 1048600
  2.6 0.0 copy-start.1
  2.6 1.0 %copy-done.1 = f32[4,2,64,256]{3,2,1,0:T(8,128)S(1)} copy-done((f32[4,2,64,256]{3,2,1,0:T(8,128)S(1)}, f32[4,2,64,256]{3,2,1,0:T(8,128)}, u32[]{:S(2)}) %copy-start.1) | copy-done | bytes 524312
  3.6 0.0 copy-start.2
  3.6 0.9 copy-done.2
  4.6 0.0 copy-start.3
  4.6 0.9 copy-done.3
  5.5 0.0 copy-start.4
  5.5 0.9 copy-done.4
  6.5 0.0 copy-start.5
  6.5 0.9 copy-done.5
  7.4 0.0 copy-start.6
  7.4 0.8 copy-done.6
  8.2 0.0 copy-start.7
  8.2 0.8 copy-done.7
  9.1 0.0 copy-start.8
  9.1 0.8 copy-done.8
  9.9 0.0 copy-start.9
  9.9 0.8 copy-done.9
  10.7 0.0 copy-start.10
  10.7 0.7 copy-done.10
  11.4 0.0 copy-start.12
  11.4 0.7 copy-done.12
  12.1 80.9 %flow.1 = (f32[16,1,32,128]{3,2,1,0:T(8,128)S(1)}, f32[16,1,32,128]{3,2,1,0:T(8,128)S(1)}, f32[1,1]{1,0:T(1,128)}) custom-call(f32[4,2,64,256]{3,2,1,0:T(8,128)S(1)} %copy-done.1, bf16[54,128]{1,0:T(8,128)(2,1)S(1)} %copy-done.12, f32[1,128]{1,0:T(1,128)S(1)} %bitcast.5, bf16[128,128]{1,0:T(8,128)(2,1)S(1)} %copy-done.9, f32[1,128]{1,0:T(1,128)S(1)} %bitcast.6, ...), custom_call_target="tpu_custom_call" | custom-call | tf_op jit(solution)/shard_map/flow/pallas_call | solution.py:527
  93.0 0.7 copy.22
  93.7 0.7 copy.23
Async XLA Ops:
  0.6 0.7 copy-start.11
  0.6 0.7 copy-start.13
  0.7 0.7 copy-start.14
  0.7 0.7 copy-start.15
  1.4 1.2 %copy-start = (bf16[2,512,512]{2,1,0:T(8,128)(2,1)S(1)}, bf16[2,512,512]{2,1,0:T(8,128)(2,1)}, u32[]{:S(2)}) copy-start(bf16[2,512,512]{2,1,0:T(8,128)(2,1)} %constant.19.clone.forward_y) | copy-start | bytes 3145732
  2.6 1.0 %copy-start.1 = (f32[4,2,64,256]{3,2,1,0:T(8,128)S(1)}, f32[4,2,64,256]{3,2,1,0:T(8,128)}, u32[]{:S(2)}) copy-start(f32[4,2,64,256]{3,2,1,0:T(8,128)} %dens.1) | copy-start | bytes 1572868
  3.6 0.9 copy-start.2
  4.6 0.9 copy-start.3
  5.5 0.9 copy-start.4
  6.5 0.9 copy-start.5
  7.4 0.8 copy-start.6
  8.2 0.8 copy-start.7
  9.1 0.8 copy-start.8
  9.9 0.8 copy-start.9
  10.7 0.7 copy-start.10
  11.4 0.7 copy-start.12

commit v2 on v1

--- a/solution.py
+++ b/solution.py
@@ -20,6 +20,8 @@
 GZ = 32
 GY = 4
 OWN_ROWS = ROWS + 2
+GROUP = 6
+GROUPS = OWN_ROWS // GROUP
 
 
 def real_basis(length):
@@ -109,14 +111,17 @@
 
 
 def flow_kernel(
-    dens, first_w, first_b, middle_w, middle_b, output_w, output_b, radial,
-    forward_x, forward_z, backward_z, forward_y, backward_x, spread, pick, squares,
+    dens_hbm, first_w_hbm, first_b_hbm, middle_w_hbm, middle_b_hbm, output_w_hbm, output_b_hbm,
+    radial_hbm, forward_x_hbm, forward_z_hbm, backward_z_hbm, forward_y_hbm, backward_x_hbm,
+    spread_hbm, pick_hbm, squares_hbm,
     factored, latent, log_density,
     lower_send, edge_send, lower_prev, lower_next, edge_recv,
     window, hidden, acc0, acc1, wide_w, w1, w2, b2, w3, ow32, profile,
     x_send, z_recv, z_send, y_recv, mixed, y_send, yb_recv, zb_send, x_recv, flat,
-    kept, sum_send, sum_gz, sum_gy, dens2,
-    halo_ssem, halo_rsem, gz_ssem, gz_rsem, gy_ssem, gy_rsem,
+    kept, first_held, last_held, sum_send, sum_send2, sum_gz, sum_gy, dens2,
+    first_w, first_b, middle_w, middle_b, output_w, output_b,
+    radial, forward_x, forward_z, backward_z, forward_y, backward_x, spread, pick, squares,
+    halo_ssem, halo_rsem, gz_ssem, gz_rsem, gy_ssem, gy_rsem, in_sem,
 ):
     me_z = lax.axis_index("gz")
     me_y = lax.axis_index("gy")
@@ -126,6 +131,45 @@
 
     def near_y(step):
         return lax.rem(me_y + step + GY, GY)
+
+    def fetch(src, dst, index):
+        copy = pltpu.make_async_copy(src, dst, in_sem.at[index])
+        copy.start()
+        return copy
+
+    lower_in = [
+        fetch(
+            dens_hbm.at[pl.ds(0, 2), :, :, pl.ds(half * 128, 128)],
+            dens2.at[half, pl.ds(0, 2)], half,
+        )
+        for half in range(2)
+    ]
+    weights_in = [
+        fetch(src, dst, 2 + i)
+        for i, (src, dst) in enumerate(
+            (
+                (first_w_hbm, first_w), (first_b_hbm, first_b), (pick_hbm, pick),
+                (middle_w_hbm, middle_w), (middle_b_hbm, middle_b), (output_w_hbm, output_w),
+            )
+        )
+    ]
+    filter_in = [fetch(radial_hbm, radial, 8), fetch(squares_hbm, squares, 9)]
+    late_in = [
+        fetch(
+            dens_hbm.at[pl.ds(2, 2), :, :, pl.ds(half * 128, 128)],
+            dens2.at[half, pl.ds(2, 2)], 10 + half,
+        )
+        for half in range(2)
+    ] + [
+        fetch(src, dst, 12 + i)
+        for i, (src, dst) in enumerate(
+            (
+                (output_b_hbm, output_b), (forward_x_hbm, forward_x), (forward_z_hbm, forward_z),
+                (forward_y_hbm, forward_y), (backward_z_hbm, backward_z),
+                (backward_x_hbm, backward_x), (spread_hbm, spread),
+            )
+        )
+    ]
 
     barrier = pltpu.get_barrier_semaphore()
 
@@ -142,16 +186,22 @@
                 barrier, inc=1, device_id=(near_z(dz), near_y(dy)), device_id_type=MESH
             )
 
+    for copy in lower_in:
+        copy.wait()
     for z in range(2):
         for c in range(2):
-            lower_send[z, c] = dens[c, z].astype(BF16)
+            for half in range(2):
+                lower_send[z, c, :, pl.ds(half * 128, 128)] = dens2[half, c, z].astype(BF16)
     for side in range(2):
         for row in range(2):
             for z in range(2):
                 for c in range(2):
                     source_row = row if side == 0 else ROWS - 2 + row
-                    line = dens[c, z, pl.ds(source_row, 1), :]
-                    edge_send[side, pl.ds(row * 4 + z * 2 + c, 1), :] = line.astype(BF16).astype(F32)
+                    for half in range(2):
+                        line = dens2[half, c, z, pl.ds(source_row, 1), :]
+                        edge_send[
+                            side, pl.ds(row * 4 + z * 2 + c, 1), pl.ds(half * 128, 128)
+                        ] = line.astype(BF16).astype(F32)
 
     pl.semaphore_wait(barrier, (GZ - 1) + (GY - 1) + 4)
 
@@ -178,9 +228,8 @@
             )
             index += 1
 
-    for half in range(2):
-        dens2[half] = dens[:, :, :, pl.ds(half * 128, 128)]
-
+    for copy in weights_in:
+        copy.wait()
     wide_w[...] = jnp.zeros_like(wide_w)
     wide_w[pl.ds(0, 54), :] = first_w[...].astype(F32)
     for piece, part in enumerate(split3(first_b[...])):
@@ -198,23 +247,6 @@
         for b in range(3):
             w3[pl.ds(b * 16, 12), pl.ds(a * 128, 128)] = ow32[pl.ds(36 * a + 12 * b, 12), :]
 
-    step_x = (me_z * 4 + me_y + 1) // 2
-    freq_x = step_x.astype(F32) * (1.0 / 128.0)
-    weights = radial[...]
-    centres = lax.broadcasted_iota(jnp.int32, (32, 512), 0).astype(F32)
-
-    def filter_part(part, carry):
-        lanes = pl.ds(pl.multiple_of(part * 512, 512), 512)
-        kappa = jnp.sqrt(squares[:, lanes] + freq_x * freq_x) * (2.0 / math.sqrt(3.0))
-        scaled = kappa * 31.0 - centres
-        basis = jnp.exp(-scaled * scaled)
-        values = mul3(split2(weights), split2(basis))
-        for j in range(4):
-            profile[pl.ds(part * 4 + j, 128, stride=32), :] = values[:, j * 128 : (j + 1) * 128]
-        return carry
-
-    lax.fori_loop(0, 8, filter_part, 0)
-
     def put(first, count, slot, values):
         for e, shifted in enumerate((shift_right(values), values, shift_left(values))):
             for half in range(2):
@@ -229,10 +261,14 @@
         window[half, pl.ds(68 * SLOTS, 36), :] = jnp.zeros((36, 128), F32)
     for z in range(2):
         for c in range(2):
-            put(2, ROWS, (z + 2) * 2 + c, dens[c, z].astype(BF16).astype(F32))
-
+            put(2, ROWS, (z + 2) * 2 + c, lower_send[z, c].astype(F32))
+
+    for copy in late_in:
+        copy.wait()
     for copy in halo:
-        copy.wait()
+        copy.wait_recv()
+    for copy in halo:
+        copy.wait_send()
 
     has_prev = me_z > 0
     has_next = me_z < GZ - 1
@@ -294,25 +330,65 @@
         for half in range(2):
             acc[half, pl.ds(0, 32), :] = jnp.zeros((32, 128), F32)
 
-    def later_planes(pair, carry):
-        for sub in range(2):
-            r = pair * 2 + 1 + sub
-            first_layer = jnp.maximum(mul(w1[pl.ds(128, 384), :], columns(r)), 0.0).astype(BF16)
+    def group_rows(group):
+        return [(sub, group * GROUP + 1 + sub) for sub in range(GROUP)]
+
+    def later_first(group):
+        for sub, r in group_rows(group):
+            values = mul(w1[pl.ds(128, 384), :], columns(r))
+            first_held[sub] = jnp.maximum(values, 0.0).astype(BF16)
+
+    def later_second(group):
+        for sub, r in group_rows(group):
+            first_layer = first_held[sub]
             layers = [second(first_layer[p * 128 : (p + 1) * 128]) for p in range(3)]
-            stacked = jnp.concatenate(layers, axis=0)
-            hidden[r] = stacked[0:256]
+            hidden[r] = jnp.concatenate(layers[0:2], axis=0)
+            last_held[sub] = layers[2]
+
+    def later_last(group):
+        for sub, r in group_rows(group):
+            stacked = jnp.concatenate([hidden[r], last_held[sub]], axis=0)
             add_taps(acc1, r, mul(w3_second, stacked))
-        return carry
-
-    def first_plane(pair, carry):
-        for sub in range(2):
-            r = pair * 2 + 1 + sub
-            first_layer = jnp.maximum(mul(w1[pl.ds(0, 128), :], columns(r)), 0.0).astype(BF16)
-            stacked = jnp.concatenate([second(first_layer), hidden[r]], axis=0)
+
+    def early_first(group):
+        for sub, r in group_rows(group):
+            values = mul(w1[pl.ds(0, 128), :], columns(r))
+            first_held[sub, pl.ds(0, 128)] = jnp.maximum(values, 0.0).astype(BF16)
+
+    def early_second(group):
+        for sub, r in group_rows(group):
+            last_held[sub] = second(first_held[sub, pl.ds(0, 128)])
+
+    def early_last(group):
+        for sub, r in group_rows(group):
+            stacked = jnp.concatenate([last_held[sub], hidden[r]], axis=0)
             add_taps(acc0, r, mul(w3_first, stacked))
-        return carry
-
-    lax.fori_loop(0, OWN_ROWS // 2, later_planes, 0)
+
+    def start_groups(first, middle, last):
+        first(0)
+        middle(0)
+        first(1)
+
+    def run_groups(first, middle, last, begin, end):
+        def step(group, carry):
+            last(group - 2)
+            middle(group - 1)
+            first(group)
+            return carry
+
+        lax.fori_loop(begin, end, step, 0)
+
+    def end_groups(first, middle, last):
+        last(GROUPS - 2)
+        middle(GROUPS - 1)
+        last(GROUPS - 1)
+
+    later = (later_first, later_second, later_last)
+    early = (early_first, early_second, early_last)
+
+    start_groups(*later)
+    run_groups(*later, 2, GROUPS)
+    end_groups(*later)
 
     def couple(acc, z, parity):
         raw = []
@@ -354,6 +430,26 @@
             total = total + values[:, at : at + 128]
         return jnp.sum(total.reshape(rows // 8, 8, 128), axis=0)
 
+    def make_filter():
+        step_x = (me_z * 4 + me_y + 1) // 2
+        freq_x = step_x.astype(F32) * (1.0 / 128.0)
+        for copy in filter_in:
+            copy.wait()
+        weights = radial[...]
+        centres = lax.broadcasted_iota(jnp.int32, (32, 512), 0).astype(F32)
+
+        def filter_part(part, carry):
+            lanes = pl.ds(pl.multiple_of(part * 512, 512), 512)
+            kappa = jnp.sqrt(squares[:, lanes] + freq_x * freq_x) * (2.0 / math.sqrt(3.0))
+            scaled = kappa * 31.0 - centres
+            basis = jnp.exp(-scaled * scaled)
+            values = mul3(split2(weights), split2(basis))
+            for j in range(4):
+                profile[pl.ds(part * 4 + j, 128, stride=32), :] = values[:, j * 128 : (j + 1) * 128]
+            return carry
+
+        lax.fori_loop(0, 8, filter_part, 0)
+
     source, scale_sum = couple(acc1, 1, 0)
     kept[0] = source
     total = fold(scale_sum)
@@ -361,6 +457,8 @@
         (forward_x[0], forward_x[1]), split2(source), ((1,), (1,))
     )
     x_send[...] = x_modes.reshape(GZ, 8, 128)
+
+    sent = []
 
     def send_all_gz(src, dst, stage):
         def one(i, carry):
@@ -380,7 +478,8 @@
             send_sem=gz_ssem.at[stage], recv_sem=gz_rsem.at[stage],
             device_id=(near_z(1), me_y), device_id_type=MESH,
         )
-        copy.wait()
+        copy.wait_recv()
+        sent.append(copy)
 
     def send_all_gy(src, dst, stage):
         for i in range(1, GY):
@@ -397,18 +496,20 @@
             send_sem=gy_ssem.at[stage], recv_sem=gy_rsem.at[stage],
             device_id=(me_z, near_y(1)), device_id_type=MESH,
         )
-        copy.wait()
+        copy.wait_recv()
+        sent.append(copy)
 
     send_all_gz(x_send, z_recv, 0)
     kept[1], scale_sum = couple(acc1, 1, 1)
     total = total + fold(scale_sum)
-    lax.fori_loop(0, 8, first_plane, 0)
+    make_filter()
     wait_all_gz(x_send, z_recv, 0)
 
     z_modes = mul3((forward_z[0], forward_z[1]), split2(z_recv[...].reshape(256, 128)))
     z_send[...] = z_modes.reshape(GY, 64, 128)
     send_all_gy(z_send, y_recv, 0)
-    lax.fori_loop(8, 16, first_plane, 0)
+    start_groups(*early)
+    run_groups(*early, 2, 6)
     wait_all_gy(z_send, y_recv, 0)
 
     lines = jnp.concatenate([y_recv[g] for g in range(GY)], axis=1)
@@ -425,7 +526,8 @@
     for g in range(GY):
         y_send[g] = back[:, g * 128 : (g + 1) * 128]
     send_all_gy(y_send, yb_recv, 1)
-    lax.fori_loop(16, 24, first_plane, 0)
+    run_groups(*early, 6, GROUPS)
+    end_groups(*early)
     wait_all_gy(y_send, yb_recv, 1)
 
     for pair in range(2):
@@ -434,7 +536,6 @@
         zb_send[:, pl.ds(pair * 8, 8), :] = planes.reshape(GZ, 8, 128)
     send_all_gz(zb_send, x_recv, 1)
 
-    lax.fori_loop(24, OWN_ROWS // 2, first_plane, 0)
     squares_sum = jnp.zeros((8, 128), F32)
     for parity in range(2):
         coupled, scale_sum = couple(acc0, 0, parity)
@@ -468,10 +569,12 @@
     send_all_gz(sum_send, sum_gz, 2)
     wait_all_gz(sum_send, sum_gz, 2)
     total = jnp.sum(sum_gz[...], axis=0)
-    sum_send[pl.ds(0, GY)] = jnp.broadcast_to(total[None], (GY, 8, 128))
-    send_all_gy(sum_send, sum_gy, 2)
-    wait_all_gy(sum_send, sum_gy, 2)
+    sum_send2[...] = jnp.broadcast_to(total[None], sum_send2.shape)
+    send_all_gy(sum_send2, sum_gy, 2)
+    wait_all_gy(sum_send2, sum_gy, 2)
     total = jnp.sum(sum_gy[...], axis=0)
+    for copy in sent:
+        copy.wait_send()
     count = 4.0 * 64 * 256 * 256
     log_density[0, 0] = jnp.sum(total) / count - 0.5 * math.log(2.0 * math.pi)
 
@@ -479,12 +582,14 @@
 def shards(consts, density_field, first_weight, first_bias, middle_weight, middle_bias, output_weight, output_bias, radial_weights):
     vmem = pl.BlockSpec(memory_space=pltpu.VMEM)
     smem = pl.BlockSpec(memory_space=pltpu.SMEM)
+    hbm = pl.BlockSpec(memory_space=pltpu.HBM)
     operands = [
         density_field, first_weight, first_bias.reshape(1, 128), middle_weight,
         middle_bias.reshape(1, 128), output_weight, output_bias, radial_weights.reshape(128, 32),
     ] + [jnp.asarray(value) for value in consts.values()]
-    specs = [vmem] * len(operands)
-    specs[6] = smem
+    specs = [hbm] * len(operands)
+    held = [pltpu.VMEM(value.shape, value.dtype) for value in operands]
+    held[6] = pltpu.SMEM(output_bias.shape, F32)
     buffers = [
         pltpu.VMEM((2, 2, ROWS, WIDE), BF16),
         pltpu.VMEM((2, 8, WIDE), F32),
@@ -513,16 +618,21 @@
         pltpu.VMEM((GZ, 16, 128), F32),
         pltpu.VMEM((512, 128), F32),
         pltpu.VMEM((2, 128, WIDE), F32),
+        pltpu.VMEM((GROUP, 384, WIDE), BF16),
+        pltpu.VMEM((GROUP, 128, WIDE), BF16),
         pltpu.VMEM((GZ, 8, 128), F32),
+        pltpu.VMEM((GY, 8, 128), F32),
         pltpu.VMEM((GZ, 8, 128), F32),
         pltpu.VMEM((GY, 8, 128), F32),
         pltpu.VMEM((2, 4, 2, ROWS, 128), F32),
+    ] + held[1:] + [
         pltpu.SemaphoreType.DMA((10,)),
         pltpu.SemaphoreType.DMA((10,)),
         pltpu.SemaphoreType.DMA((3,)),
         pltpu.SemaphoreType.DMA((3,)),
         pltpu.SemaphoreType.DMA((3,)),
         pltpu.SemaphoreType.DMA((3,)),
+        pltpu.SemaphoreType.DMA((19,)),
     ]
     factored, latent, log_density = pl.pallas_call(
         flow_kernel,
@@ -535,7 +645,7 @@
         out_specs=(vmem, vmem, smem),
         scratch_shapes=buffers,
         compiler_params=pltpu.CompilerParams(
-            collective_id=0, has_side_effects=True, vmem_limit_bytes=48 * 1024 * 1024
+            collective_id=0, has_side_effects=True, vmem_limit_bytes=60 * 1024 * 1024
         ),
         name="flow",
     )(*operands)

time: 96.9 us -> 67.6 us (0.70)
  Pallas kernels: 80.9 us -> 62.6 us
  local copies, waits for them, and re-layouts: 12.8 us -> 2.42 us
    pallas_call x1, Pallas kernels: 80.9 us -> 62.6 us  [shards(): pl.pallas_call(flow_kernel, out_shape=(jax.ShapeDtypeStruct((16, 1, 32, 1...]
    unnamed x34 -> x4, local copies, waits for them, and re-layouts: 12.8 us -> 2.42 us
where the time goes in v2:
time: 67.6 us; the launch traced here: 67.5 us
  Pallas kernels  62.6 us (93%)
  local copies, waits for them, and re-layouts  2.42 us (4%)
  between operations  2.42 us (4%)
    pallas_call x1, Pallas kernels, shards(): pl.pallas_call(flow_kernel, out_shape=(jax.ShapeDtypeStruct((16, 1, 32, 1...  62.6 us
    unnamed x4, local copies, waits for them, and re-layouts  2.42 us

profile of v2, /device:TPU:1, one launch (start us, length us, event | category | flops | bytes accessed | tf_op | source)
XLA Modules:
  0.0 67.5 jit_solution(126582622479649817)
XLA Ops:
  0.6 62.6 %flow.1 = (f32[16,1,32,128]{3,2,1,0:T(8,128)}, f32[16,1,32,128]{3,2,1,0:T(8,128)}, f32[1,1]{1,0:T(1,128)}) custom-call(f32[4,2,64,256]{3,2,1,0:T(8,128)} %dens_hbm.1, bf16[54,128]{1,0:T(8,128)(2,1)} %first_w_hbm.1, f32[1,128]{1,0:T(1,128)} %bitcast.5, bf16[128,128]{1,0:T(8,128)(2,1)} %middle_w_hbm.1, f32[1,128]{1,0:T(1,128)} %bitcast.6, ...), custom_call_target="tpu_custom_call" | custom-call | tf_op jit(solution)/shard_map/flow/pallas_call | solution.py:637
  63.3 0.0 copy-start
  63.3 1.7 %copy.22 = f32[16,1,32,128]{3,2,1,0:T(8,128)} copy(f32[16,1,32,128]{3,2,1,0:T(8,128)} %get-tuple-element.12) | data formatting | bytes 524288
  65.0 0.0 copy-done
  65.0 0.7 %copy.23 = f32[16,1,32,128]{3,2,1,0:T(8,128)} copy(f32[16,1,32,128]{3,2,1,0:T(8,128)S(1)} %copy-done) | data formatting | bytes 524288
Async XLA Ops:
  63.3 1.7 %copy-start = (f32[16,1,32,128]{3,2,1,0:T(8,128)S(1)}, f32[16,1,32,128]{3,2,1,0:T(8,128)}, u32[]{:S(2)}) copy-start(f32[16,1,32,128]{3,2,1,0:T(8,128)} %get-tuple-element.13) | copy-start | bytes 786436

commit v3 on v2

--- a/solution.py
+++ b/solution.py
@@ -11,6 +11,7 @@
 from jax.sharding import PartitionSpec as P
 
 MESH = pl.DeviceIdType.MESH
+LOGICAL = pl.DeviceIdType.LOGICAL
 F32 = jnp.float32
 BF16 = jnp.bfloat16
 
@@ -19,6 +20,7 @@
 WIDE = 256
 GZ = 32
 GY = 4
+COUNT = GZ * GY
 OWN_ROWS = ROWS + 2
 GROUP = 6
 GROUPS = OWN_ROWS // GROUP
@@ -117,21 +119,32 @@
     factored, latent, log_density,
     lower_send, edge_send, lower_prev, lower_next, edge_recv,
     window, hidden, acc0, acc1, wide_w, w1, w2, b2, w3, ow32, profile,
-    x_send, z_recv, z_send, y_recv, mixed, y_send, yb_recv, zb_send, x_recv, flat,
-    kept, first_held, last_held, sum_send, sum_send2, sum_gz, sum_gy, dens2,
+    x_send, z_recv, mixed, zb_send, x_recv,
+    kept, first_held, last_held, sum_send, sum_recv, dens2,
     first_w, first_b, middle_w, middle_b, output_w, output_b,
     radial, forward_x, forward_z, backward_z, forward_y, backward_x, spread, pick, squares,
-    halo_ssem, halo_rsem, gz_ssem, gz_rsem, gy_ssem, gy_rsem, in_sem,
+    halo_ssem, halo_rsem, all_ssem, all_rsem, in_sem,
 ):
     me_z = lax.axis_index("gz")
     me_y = lax.axis_index("gy")
 
+    me = me_z * GY + me_y
+
+    def near(step):
+        return lax.rem(me + step, COUNT)
+
     def near_z(step):
         return lax.rem(me_z + step + GZ, GZ)
 
     def near_y(step):
         return lax.rem(me_y + step + GY, GY)
 
+    barrier = pltpu.get_barrier_semaphore()
+    sides = [(dz, dy) for dz in (-1, 0, 1) for dy in (-1, 0, 1) if (dz, dy) != (0, 0)]
+    for dz, dy in sides:
+        pl.semaphore_signal(
+            barrier, inc=1, device_id=(near_z(dz), near_y(dy)), device_id_type=MESH
+        )
     def fetch(src, dst, index):
         copy = pltpu.make_async_copy(src, dst, in_sem.at[index])
         copy.start()
@@ -144,47 +157,12 @@
         )
         for half in range(2)
     ]
-    weights_in = [
-        fetch(src, dst, 2 + i)
-        for i, (src, dst) in enumerate(
-            (
-                (first_w_hbm, first_w), (first_b_hbm, first_b), (pick_hbm, pick),
-                (middle_w_hbm, middle_w), (middle_b_hbm, middle_b), (output_w_hbm, output_w),
-            )
-        )
-    ]
-    filter_in = [fetch(radial_hbm, radial, 8), fetch(squares_hbm, squares, 9)]
-    late_in = [
-        fetch(
-            dens_hbm.at[pl.ds(2, 2), :, :, pl.ds(half * 128, 128)],
-            dens2.at[half, pl.ds(2, 2)], 10 + half,
-        )
-        for half in range(2)
-    ] + [
-        fetch(src, dst, 12 + i)
-        for i, (src, dst) in enumerate(
-            (
-                (output_b_hbm, output_b), (forward_x_hbm, forward_x), (forward_z_hbm, forward_z),
-                (forward_y_hbm, forward_y), (backward_z_hbm, backward_z),
-                (backward_x_hbm, backward_x), (spread_hbm, spread),
-            )
-        )
-    ]
-
-    barrier = pltpu.get_barrier_semaphore()
-
-    def greet_z(i, carry):
-        pl.semaphore_signal(barrier, inc=1, device_id=(near_z(i), me_y), device_id_type=MESH)
+
+    def greet(i, carry):
+        pl.semaphore_signal(barrier, inc=1, device_id=near(i), device_id_type=LOGICAL)
         return carry
 
-    lax.fori_loop(1, GZ, greet_z, 0)
-    for i in range(1, GY):
-        pl.semaphore_signal(barrier, inc=1, device_id=(me_z, near_y(i)), device_id_type=MESH)
-    for dz in (-1, 1):
-        for dy in (-1, 1):
-            pl.semaphore_signal(
-                barrier, inc=1, device_id=(near_z(dz), near_y(dy)), device_id_type=MESH
-            )
+    lax.fori_loop(1, COUNT, greet, 0)
 
     for copy in lower_in:
         copy.wait()
@@ -203,7 +181,7 @@
                             side, pl.ds(row * 4 + z * 2 + c, 1), pl.ds(half * 128, 128)
                         ] = line.astype(BF16).astype(F32)
 
-    pl.semaphore_wait(barrier, (GZ - 1) + (GY - 1) + 4)
+    pl.semaphore_wait(barrier, COUNT - 1 + len(sides))
 
     halo = []
 
@@ -215,18 +193,45 @@
         copy.start()
         halo.append(copy)
 
-    send_halo(lower_send.at[1], lower_prev.at[1], 0, (near_z(1), me_y))
-    send_halo(lower_send.at[0], lower_next.at[0], 1, (near_z(-1), me_y))
-    send_halo(lower_send.at[1], lower_next.at[1], 2, (near_z(-1), me_y))
-    send_halo(lower_send.at[0], lower_prev.at[0], 3, (near_z(1), me_y))
-    index = 4
+    index = 0
     for side in range(2):
         to_y = near_y(-1) if side == 0 else near_y(1)
-        for dz in (-1, 0, 1):
+        for dz in (-1, 1, 0):
             send_halo(
                 edge_send.at[side], edge_recv.at[1 - side, 1 - dz], index, (near_z(dz), to_y)
             )
             index += 1
+    send_halo(lower_send.at[1], lower_prev.at[1], 6, (near_z(1), me_y))
+    send_halo(lower_send.at[0], lower_next.at[0], 7, (near_z(-1), me_y))
+    send_halo(lower_send.at[1], lower_next.at[1], 8, (near_z(-1), me_y))
+    send_halo(lower_send.at[0], lower_prev.at[0], 9, (near_z(1), me_y))
+
+    weights_in = [
+        fetch(src, dst, 2 + i)
+        for i, (src, dst) in enumerate(
+            (
+                (first_w_hbm, first_w), (first_b_hbm, first_b), (pick_hbm, pick),
+                (middle_w_hbm, middle_w), (middle_b_hbm, middle_b), (output_w_hbm, output_w),
+            )
+        )
+    ]
+    filter_in = [fetch(radial_hbm, radial, 8), fetch(squares_hbm, squares, 9)]
+    late_in = [
+        fetch(
+            dens_hbm.at[pl.ds(2, 2), :, :, pl.ds(half * 128, 128)],
+            dens2.at[half, pl.ds(2, 2)], 10 + half,
+        )
+        for half in range(2)
+    ] + [
+        fetch(src, dst, 12 + i)
+        for i, (src, dst) in enumerate(
+            (
+                (output_b_hbm, output_b), (forward_x_hbm, forward_x), (forward_z_hbm, forward_z),
+                (forward_y_hbm, forward_y), (backward_z_hbm, backward_z),
+                (backward_x_hbm, backward_x), (spread_hbm, spread),
+            )
+        )
+    ]
 
     for copy in weights_in:
         copy.wait()
@@ -259,16 +264,35 @@
         for slot in range(37, 40):
             window[half, pl.ds(slot, 72, stride=SLOTS), :] = jnp.zeros((72, 128), F32)
         window[half, pl.ds(68 * SLOTS, 36), :] = jnp.zeros((36, 128), F32)
+        for slot in (0, 1, 12, 13, 24, 25):
+            window[half, pl.ds(2 * SLOTS + slot, ROWS, stride=SLOTS), :] = jnp.zeros((ROWS, 128), F32)
     for z in range(2):
         for c in range(2):
             put(2, ROWS, (z + 2) * 2 + c, lower_send[z, c].astype(F32))
 
+    step_x = (me + 1) // 2
+    freq_x = step_x.astype(F32) * (1.0 / 128.0)
+    for copy in filter_in:
+        copy.wait()
+    weights = radial[...]
+    centres = lax.broadcasted_iota(jnp.int32, (32, 512), 0).astype(F32)
+
+    def filter_part(part, carry):
+        lanes = pl.ds(pl.multiple_of(part * 512, 512), 512)
+        kappa = jnp.sqrt(squares[:, lanes] + freq_x * freq_x) * (2.0 / math.sqrt(3.0))
+        scaled = kappa * 31.0 - centres
+        basis = jnp.exp(-scaled * scaled)
+        values = mul3(split2(weights), split2(basis))
+        for j in range(4):
+            profile[pl.ds(part * 4 + j, 128, stride=32), :] = values[:, j * 128 : (j + 1) * 128]
+        return carry
+
+    lax.fori_loop(0, 8, filter_part, 0)
+
     for copy in late_in:
         copy.wait()
-    for copy in halo:
+    for copy in halo[:9]:
         copy.wait_recv()
-    for copy in halo:
-        copy.wait_send()
 
     has_prev = me_z > 0
     has_next = me_z < GZ - 1
@@ -276,7 +300,8 @@
     has_down = me_y < GY - 1
     for z in range(2):
         for c in range(2):
-            put(2, ROWS, z * 2 + c, jnp.where(has_prev, lower_prev[z, c].astype(F32), 0.0))
+            if z == 1:
+                put(2, ROWS, z * 2 + c, jnp.where(has_prev, lower_prev[z, c].astype(F32), 0.0))
             put(2, ROWS, (z + 4) * 2 + c, jnp.where(has_next, lower_next[z, c].astype(F32), 0.0))
     for side in range(2):
         for offset in range(3):
@@ -430,89 +455,50 @@
             total = total + values[:, at : at + 128]
         return jnp.sum(total.reshape(rows // 8, 8, 128), axis=0)
 
-    def make_filter():
-        step_x = (me_z * 4 + me_y + 1) // 2
-        freq_x = step_x.astype(F32) * (1.0 / 128.0)
-        for copy in filter_in:
-            copy.wait()
-        weights = radial[...]
-        centres = lax.broadcasted_iota(jnp.int32, (32, 512), 0).astype(F32)
-
-        def filter_part(part, carry):
-            lanes = pl.ds(pl.multiple_of(part * 512, 512), 512)
-            kappa = jnp.sqrt(squares[:, lanes] + freq_x * freq_x) * (2.0 / math.sqrt(3.0))
-            scaled = kappa * 31.0 - centres
-            basis = jnp.exp(-scaled * scaled)
-            values = mul3(split2(weights), split2(basis))
-            for j in range(4):
-                profile[pl.ds(part * 4 + j, 128, stride=32), :] = values[:, j * 128 : (j + 1) * 128]
-            return carry
-
-        lax.fori_loop(0, 8, filter_part, 0)
-
     source, scale_sum = couple(acc1, 1, 0)
     kept[0] = source
     total = fold(scale_sum)
     x_modes = mul3(
         (forward_x[0], forward_x[1]), split2(source), ((1,), (1,))
     )
-    x_send[...] = x_modes.reshape(GZ, 8, 128)
-
-    sent = []
-
-    def send_all_gz(src, dst, stage):
+    x_send[...] = x_modes.reshape(COUNT, 2, 128)
+
+    sent = list(halo)
+
+    def send_all(part, dst, stage):
         def one(i, carry):
-            to = near_z(i)
+            to = near(i)
             pltpu.make_async_remote_copy(
-                src_ref=src.at[to], dst_ref=dst.at[me_z], send_sem=gz_ssem.at[stage], recv_sem=gz_rsem.at[stage],
-                device_id=(to, me_y), device_id_type=MESH,
+                src_ref=part(to), dst_ref=dst.at[me], send_sem=all_ssem.at[stage],
+                recv_sem=all_rsem.at[stage], device_id=to, device_id_type=LOGICAL,
             ).start()
             return carry
 
-        lax.fori_loop(1, GZ, one, 0)
-        dst[me_z] = src[me_z]
-
-    def wait_all_gz(src, dst, stage):
+        lax.fori_loop(1, COUNT, one, 0)
+        dst[me] = part(me)[...]
+
+    def wait_all(dst, stage):
         copy = pltpu.make_async_remote_copy(
-            src_ref=src.at[pl.ds(0, GZ - 1)], dst_ref=dst.at[pl.ds(0, GZ - 1)],
-            send_sem=gz_ssem.at[stage], recv_sem=gz_rsem.at[stage],
-            device_id=(near_z(1), me_y), device_id_type=MESH,
+            src_ref=dst.at[pl.ds(0, COUNT - 1)], dst_ref=dst.at[pl.ds(0, COUNT - 1)],
+            send_sem=all_ssem.at[stage], recv_sem=all_rsem.at[stage],
+            device_id=near(1), device_id_type=LOGICAL,
         )
         copy.wait_recv()
         sent.append(copy)
 
-    def send_all_gy(src, dst, stage):
-        for i in range(1, GY):
-            to = near_y(i)
-            pltpu.make_async_remote_copy(
-                src_ref=src.at[to], dst_ref=dst.at[me_y], send_sem=gy_ssem.at[stage], recv_sem=gy_rsem.at[stage],
-                device_id=(me_z, to), device_id_type=MESH,
-            ).start()
-        dst[me_y] = src[me_y]
-
-    def wait_all_gy(src, dst, stage):
-        copy = pltpu.make_async_remote_copy(
-            src_ref=src.at[pl.ds(0, GY - 1)], dst_ref=dst.at[pl.ds(0, GY - 1)],
-            send_sem=gy_ssem.at[stage], recv_sem=gy_rsem.at[stage],
-            device_id=(me_z, near_y(1)), device_id_type=MESH,
-        )
-        copy.wait_recv()
-        sent.append(copy)
-
-    send_all_gz(x_send, z_recv, 0)
+    send_all(lambda to: x_send.at[to], z_recv, 0)
     kept[1], scale_sum = couple(acc1, 1, 1)
     total = total + fold(scale_sum)
-    make_filter()
-    wait_all_gz(x_send, z_recv, 0)
-
-    z_modes = mul3((forward_z[0], forward_z[1]), split2(z_recv[...].reshape(256, 128)))
-    z_send[...] = z_modes.reshape(GY, 64, 128)
-    send_all_gy(z_send, y_recv, 0)
+    halo[9].wait_recv()
+    for c in range(2):
+        put(2, ROWS, c, jnp.where(has_prev, lower_prev[0, c].astype(F32), 0.0))
     start_groups(*early)
     run_groups(*early, 2, 6)
-    wait_all_gy(z_send, y_recv, 0)
-
-    lines = jnp.concatenate([y_recv[g] for g in range(GY)], axis=1)
+    wait_all(z_recv, 0)
+
+    z_modes = mul3((forward_z[0], forward_z[1]), split2(z_recv[...].reshape(256, 128)))
+
+    lines = jnp.concatenate([z_modes[g * 64 : (g + 1) * 64] for g in range(GY)], axis=1)
     modes = mul3(split2(lines), (forward_y[0], forward_y[1]))
     parts = [
         modes[k * 32 : (k + 1) * 32, c * 128 : (c + 1) * 128] for k in range(2) for c in range(4)
@@ -523,18 +509,16 @@
             value = value + profile[pl.ds(o * 256 + c * 32, 32), :] * parts[c]
         mixed[pl.ds((o // 4) * 32, 32), pl.ds((o % 4) * 128, 128)] = value
     back = mul3(split2(mixed[...]), (forward_y[0], forward_y[1]), ((1,), (1,)))
-    for g in range(GY):
-        y_send[g] = back[:, g * 128 : (g + 1) * 128]
-    send_all_gy(y_send, yb_recv, 1)
+    for pair in range(2):
+        lines = jnp.concatenate(
+            [back[:, g * 128 : (g + 1) * 128] for g in (2 * pair, 2 * pair + 1)], axis=0
+        )
+        planes = mul3((backward_z[0], backward_z[1]), split2(lines))
+        zb_send[:, pl.ds(pair * 2, 2)] = planes.reshape(GZ, 2, 4, 128)
+
+    send_all(lambda to: zb_send.at[to // GY, lax.rem(to, GY)], x_recv, 1)
     run_groups(*early, 6, GROUPS)
     end_groups(*early)
-    wait_all_gy(y_send, yb_recv, 1)
-
-    for pair in range(2):
-        lines = yb_recv[pl.ds(pair * 2, 2)].reshape(256, 128)
-        planes = mul3((backward_z[0], backward_z[1]), split2(lines))
-        zb_send[:, pl.ds(pair * 8, 8), :] = planes.reshape(GZ, 8, 128)
-    send_all_gz(zb_send, x_recv, 1)
 
     squares_sum = jnp.zeros((8, 128), F32)
     for parity in range(2):
@@ -550,12 +534,11 @@
     for k in range(2):
         latent[pl.ds(k * 4, 4), 0] = source[:, k * 128 : (k + 1) * 128].reshape(4, 32, 128)
     target = spread_x(kept[1])
-    wait_all_gz(zb_send, x_recv, 1)
-
-    flat[...] = x_recv[...].reshape(512, 128)
+    wait_all(x_recv, 1)
+
     shifts = []
     for og in range(4):
-        lines = flat[pl.ds(og, 128, stride=4), :]
+        lines = x_recv[:, og, :]
         shifts.append(jnp.transpose(mul3((backward_x[0], backward_x[1]), split2(lines))))
     for k in range(2):
         scale = jnp.tanh(shifts[k])
@@ -565,14 +548,11 @@
         latent[pl.ds(8 + k * 4, 4), 0] = moved.reshape(4, 32, 128)
 
     total = total - 0.5 * squares_sum
-    sum_send[...] = jnp.broadcast_to(total[None], sum_send.shape)
-    send_all_gz(sum_send, sum_gz, 2)
-    wait_all_gz(sum_send, sum_gz, 2)
-    total = jnp.sum(sum_gz[...], axis=0)
-    sum_send2[...] = jnp.broadcast_to(total[None], sum_send2.shape)
-    send_all_gy(sum_send2, sum_gy, 2)
-    wait_all_gy(sum_send2, sum_gy, 2)
-    total = jnp.sum(sum_gy[...], axis=0)
+    sum_send[0] = jnp.sum(total, axis=0, keepdims=True)
+
+    send_all(lambda to: sum_send.at[0], sum_recv, 2)
+    wait_all(sum_recv, 2)
+    total = jnp.sum(sum_recv[...], axis=0)
     for copy in sent:
         copy.wait_send()
     count = 4.0 * 64 * 256 * 256
@@ -607,29 +587,20 @@
         pltpu.VMEM((48, 384), F32),
         pltpu.VMEM((108, 128), F32),
         pltpu.VMEM((128 * 32, 128), F32),
-        pltpu.VMEM((GZ, 8, 128), F32),
-        pltpu.VMEM((GZ, 8, 128), F32),
-        pltpu.VMEM((GY, 64, 128), F32),
-        pltpu.VMEM((GY, 64, 128), F32),
+        pltpu.VMEM((COUNT, 2, 128), F32),
+        pltpu.VMEM((COUNT, 2, 128), F32),
         pltpu.VMEM((128, 512), F32),
-        pltpu.VMEM((GY, 128, 128), F32),
-        pltpu.VMEM((GY, 128, 128), F32),
-        pltpu.VMEM((GZ, 16, 128), F32),
-        pltpu.VMEM((GZ, 16, 128), F32),
-        pltpu.VMEM((512, 128), F32),
+        pltpu.VMEM((GZ, GY, 4, 128), F32),
+        pltpu.VMEM((COUNT, 4, 128), F32),
         pltpu.VMEM((2, 128, WIDE), F32),
         pltpu.VMEM((GROUP, 384, WIDE), BF16),
         pltpu.VMEM((GROUP, 128, WIDE), BF16),
-        pltpu.VMEM((GZ, 8, 128), F32),
-        pltpu.VMEM((GY, 8, 128), F32),
-        pltpu.VMEM((GZ, 8, 128), F32),
-        pltpu.VMEM((GY, 8, 128), F32),
+        pltpu.VMEM((1, 1, 128), F32),
+        pltpu.VMEM((COUNT, 1, 128), F32),
         pltpu.VMEM((2, 4, 2, ROWS, 128), F32),
     ] + held[1:] + [
         pltpu.SemaphoreType.DMA((10,)),
         pltpu.SemaphoreType.DMA((10,)),
-        pltpu.SemaphoreType.DMA((3,)),
-        pltpu.SemaphoreType.DMA((3,)),
         pltpu.SemaphoreType.DMA((3,)),
         pltpu.SemaphoreType.DMA((3,)),
         pltpu.SemaphoreType.DMA((19,)),

time: 67.6 us -> 59.6 us (0.88)
  Pallas kernels: 62.6 us -> 54.6 us
    pallas_call x1, Pallas kernels: 62.6 us -> 54.6 us  [shards(): pl.pallas_call(flow_kernel, out_shape=(jax.ShapeDtypeStruct((16, 1, 32, 1...]
where the time goes in v3:
time: 59.6 us; the launch traced here: 59.4 us
  Pallas kernels  54.6 us (92%)
  local copies, waits for them, and re-layouts  2.42 us (4%)
  between operations  2.42 us (4%)
    pallas_call x1, Pallas kernels, shards(): pl.pallas_call(flow_kernel, out_shape=(jax.ShapeDtypeStruct((16, 1, 32, 1...  54.6 us
    unnamed x4, local copies, waits for them, and re-layouts  2.42 us

profile of v3, /device:TPU:1, one launch (start us, length us, event | category | flops | bytes accessed | tf_op | source)
XLA Modules:
  0.0 59.4 jit_solution(3732081080421302198)
XLA Ops:
  0.6 54.6 %flow.1 = (f32[16,1,32,128]{3,2,1,0:T(8,128)}, f32[16,1,32,128]{3,2,1,0:T(8,128)}, f32[1,1]{1,0:T(1,128)}) custom-call(f32[4,2,64,256]{3,2,1,0:T(8,128)} %dens_hbm.1, bf16[54,128]{1,0:T(8,128)(2,1)} %first_w_hbm.1, f32[1,128]{1,0:T(1,128)} %bitcast.5, bf16[128,128]{1,0:T(8,128)(2,1)} %middle_w_hbm.1, f32[1,128]{1,0:T(1,128)} %bitcast.6, ...), custom_call_target="tpu_custom_call" | custom-call | tf_op jit(solution)/shard_map/flow/pallas_call | solution.py:608
  55.2 0.0 copy-start
  55.2 1.7 %copy.22 = f32[16,1,32,128]{3,2,1,0:T(8,128)} copy(f32[16,1,32,128]{3,2,1,0:T(8,128)} %get-tuple-element.12) | data formatting | bytes 524288
  56.9 0.0 copy-done
  56.9 0.7 %copy.23 = f32[16,1,32,128]{3,2,1,0:T(8,128)} copy(f32[16,1,32,128]{3,2,1,0:T(8,128)S(1)} %copy-done) | data formatting | bytes 524288
Async XLA Ops:
  55.2 1.7 %copy-start = (f32[16,1,32,128]{3,2,1,0:T(8,128)S(1)}, f32[16,1,32,128]{3,2,1,0:T(8,128)}, u32[]{:S(2)}) copy-start(f32[16,1,32,128]{3,2,1,0:T(8,128)} %get-tuple-element.13) | copy-start | bytes 786436

commit v4 on v3

--- a/solution.py
+++ b/solution.py
@@ -22,6 +22,8 @@
 GY = 4
 COUNT = GZ * GY
 OWN_ROWS = ROWS + 2
+CHUNK = 16
+CHUNKS = ROWS // CHUNK
 GROUP = 6
 GROUPS = OWN_ROWS // GROUP
 
@@ -185,26 +187,47 @@
 
     halo = []
 
-    def send_halo(src, dst, index, to):
-        copy = pltpu.make_async_remote_copy(
+    def halo_copy(src, dst, index, to):
+        return pltpu.make_async_remote_copy(
             src_ref=src, dst_ref=dst, send_sem=halo_ssem.at[index], recv_sem=halo_rsem.at[index],
             device_id=to, device_id_type=MESH,
         )
-        copy.start()
-        halo.append(copy)
-
-    index = 0
-    for side in range(2):
-        to_y = near_y(-1) if side == 0 else near_y(1)
-        for dz in (-1, 1, 0):
-            send_halo(
-                edge_send.at[side], edge_recv.at[1 - side, 1 - dz], index, (near_z(dz), to_y)
+
+    def chunk_copies(chunk):
+        rows = pl.ds(pl.multiple_of(chunk * CHUNK, CHUNK), CHUNK)
+        return (
+            halo_copy(
+                lower_send.at[:, :, rows], lower_next.at[:, :, rows], 6 + chunk,
+                (near_z(-1), me_y),
+            ),
+            halo_copy(
+                lower_send.at[1, :, rows], lower_prev.at[1, :, rows], 10 + chunk,
+                (near_z(1), me_y),
+            ),
+        )
+
+    def start_halo(copies):
+        for copy in copies:
+            copy.start()
+            halo.append(copy)
+
+    edges = [
+        [
+            halo_copy(
+                edge_send.at[side], edge_recv.at[1 - side, 1 - dz], side * 3 + dz + 1,
+                (near_z(dz), near_y(-1) if side == 0 else near_y(1)),
             )
-            index += 1
-    send_halo(lower_send.at[1], lower_prev.at[1], 6, (near_z(1), me_y))
-    send_halo(lower_send.at[0], lower_next.at[0], 7, (near_z(-1), me_y))
-    send_halo(lower_send.at[1], lower_next.at[1], 8, (near_z(-1), me_y))
-    send_halo(lower_send.at[0], lower_prev.at[0], 9, (near_z(1), me_y))
+            for dz in (-1, 0, 1)
+        ]
+        for side in range(2)
+    ]
+    far_plane = halo_copy(lower_send.at[0], lower_prev.at[0], 14, (near_z(1), me_y))
+    start_halo(edges[1])
+    start_halo(chunk_copies(0))
+    start_halo(edges[0])
+    for chunk in range(1, CHUNKS):
+        start_halo(chunk_copies(chunk))
+    start_halo([far_plane])
 
     weights_in = [
         fetch(src, dst, 2 + i)
@@ -291,19 +314,27 @@
 
     for copy in late_in:
         copy.wait()
-    for copy in halo[:9]:
-        copy.wait_recv()
 
     has_prev = me_z > 0
     has_next = me_z < GZ - 1
     has_up = me_y > 0
     has_down = me_y < GY - 1
-    for z in range(2):
+
+    def fill_chunk(chunk):
+        for copy in chunk_copies(chunk):
+            copy.wait_recv()
+        rows = pl.ds(pl.multiple_of(chunk * CHUNK, CHUNK), CHUNK)
+        first = 2 + chunk * CHUNK
         for c in range(2):
-            if z == 1:
-                put(2, ROWS, z * 2 + c, jnp.where(has_prev, lower_prev[z, c].astype(F32), 0.0))
-            put(2, ROWS, (z + 4) * 2 + c, jnp.where(has_next, lower_next[z, c].astype(F32), 0.0))
-    for side in range(2):
+            values = lower_prev[1, c, rows, :].astype(F32)
+            put(first, CHUNK, 2 + c, jnp.where(has_prev, values, 0.0))
+            for z in range(2):
+                values = lower_next[z, c, rows, :].astype(F32)
+                put(first, CHUNK, (z + 4) * 2 + c, jnp.where(has_next, values, 0.0))
+
+    def fill_edge(side):
+        for copy in edges[1 - side]:
+            copy.wait_recv()
         for offset in range(3):
             valid = has_up if side == 0 else has_down
             if offset == 0:
@@ -320,6 +351,9 @@
                             :, half * 128 : (half + 1) * 128
                         ]
 
+    fill_edge(0)
+    fill_chunk(0)
+
     w3_lane = lax.broadcasted_iota(jnp.int32, (48, 384), 1)
     w3_first = jnp.where(jnp.logical_and(w3_lane < 128, me_z == 0), 0.0, w3[...]).astype(BF16)
     w3_second = jnp.where(
@@ -394,8 +428,9 @@
         middle(0)
         first(1)
 
-    def run_groups(first, middle, last, begin, end):
+    def run_groups(first, middle, last, begin, end, beside=lambda group: None):
         def step(group, carry):
+            beside(group)
             last(group - 2)
             middle(group - 1)
             first(group)
@@ -412,7 +447,14 @@
     early = (early_first, early_second, early_last)
 
     start_groups(*later)
-    run_groups(*later, 2, GROUPS)
+    fill_edge(1)
+
+    def later_chunk(chunk, carry):
+        fill_chunk(chunk)
+        run_groups(*later, 3 * chunk - 1, 3 * chunk + 2)
+        return carry
+
+    lax.fori_loop(1, CHUNKS, later_chunk, 0)
     end_groups(*later)
 
     def couple(acc, z, parity):
@@ -465,16 +507,19 @@
 
     sent = list(halo)
 
-    def send_all(part, dst, stage):
+    def send_one(part, dst, stage, step):
+        to = near(step)
+        pltpu.make_async_remote_copy(
+            src_ref=part(to), dst_ref=dst.at[me], send_sem=all_ssem.at[stage],
+            recv_sem=all_rsem.at[stage], device_id=to, device_id_type=LOGICAL,
+        ).start()
+
+    def send_all(part, dst, stage, end=COUNT):
         def one(i, carry):
-            to = near(i)
-            pltpu.make_async_remote_copy(
-                src_ref=part(to), dst_ref=dst.at[me], send_sem=all_ssem.at[stage],
-                recv_sem=all_rsem.at[stage], device_id=to, device_id_type=LOGICAL,
-            ).start()
+            send_one(part, dst, stage, i)
             return carry
 
-        lax.fori_loop(1, COUNT, one, 0)
+        lax.fori_loop(1, end, one, 0)
         dst[me] = part(me)[...]
 
     def wait_all(dst, stage):
@@ -486,14 +531,25 @@
         copy.wait_recv()
         sent.append(copy)
 
-    send_all(lambda to: x_send.at[to], z_recv, 0)
-    kept[1], scale_sum = couple(acc1, 1, 1)
-    total = total + fold(scale_sum)
-    halo[9].wait_recv()
+    def x_part(to):
+        return x_send.at[to]
+
+    each = (COUNT - 1) // (GROUPS - 2)
+    before = COUNT - each * (GROUPS - 2)
+
+    def send_some(group):
+        for i in range(each):
+            send_one(x_part, z_recv, 0, before + (group - 2) * each + i)
+
+    send_all(x_part, z_recv, 0, before)
+    far_plane.wait_recv()
     for c in range(2):
         put(2, ROWS, c, jnp.where(has_prev, lower_prev[0, c].astype(F32), 0.0))
     start_groups(*early)
-    run_groups(*early, 2, 6)
+    run_groups(*early, 2, GROUPS, send_some)
+    end_groups(*early)
+    kept[1], scale_sum = couple(acc1, 1, 1)
+    total = total + fold(scale_sum)
     wait_all(z_recv, 0)
 
     z_modes = mul3((forward_z[0], forward_z[1]), split2(z_recv[...].reshape(256, 128)))
@@ -517,22 +573,13 @@
         zb_send[:, pl.ds(pair * 2, 2)] = planes.reshape(GZ, 2, 4, 128)
 
     send_all(lambda to: zb_send.at[to // GY, lax.rem(to, GY)], x_recv, 1)
-    run_groups(*early, 6, GROUPS)
-    end_groups(*early)
-
-    squares_sum = jnp.zeros((8, 128), F32)
+
+    squares_sum = fold(kept[0] * kept[0])
     for parity in range(2):
         coupled, scale_sum = couple(acc0, 0, parity)
+        kept[2 + parity] = coupled
         total = total + fold(scale_sum)
         squares_sum = squares_sum + fold(coupled * coupled)
-        coupled = spread_x(coupled)
-        for k in range(2):
-            at = (2 * parity + k) * 4
-            factored[pl.ds(at, 4), 0] = coupled[:, k * 128 : (k + 1) * 128].reshape(4, 32, 128)
-    source = spread_x(kept[0])
-    squares_sum = squares_sum + fold(source * source)
-    for k in range(2):
-        latent[pl.ds(k * 4, 4), 0] = source[:, k * 128 : (k + 1) * 128].reshape(4, 32, 128)
     target = spread_x(kept[1])
     wait_all(x_recv, 1)
 
@@ -551,6 +598,14 @@
     sum_send[0] = jnp.sum(total, axis=0, keepdims=True)
 
     send_all(lambda to: sum_send.at[0], sum_recv, 2)
+    for parity in range(2):
+        coupled = spread_x(kept[2 + parity])
+        for k in range(2):
+            at = (2 * parity + k) * 4
+            factored[pl.ds(at, 4), 0] = coupled[:, k * 128 : (k + 1) * 128].reshape(4, 32, 128)
+    source = spread_x(kept[0])
+    for k in range(2):
+        latent[pl.ds(k * 4, 4), 0] = source[:, k * 128 : (k + 1) * 128].reshape(4, 32, 128)
     wait_all(sum_recv, 2)
     total = jnp.sum(sum_recv[...], axis=0)
     for copy in sent:
@@ -592,15 +647,15 @@
         pltpu.VMEM((128, 512), F32),
         pltpu.VMEM((GZ, GY, 4, 128), F32),
         pltpu.VMEM((COUNT, 4, 128), F32),
-        pltpu.VMEM((2, 128, WIDE), F32),
+        pltpu.VMEM((4, 128, WIDE), F32),
         pltpu.VMEM((GROUP, 384, WIDE), BF16),
         pltpu.VMEM((GROUP, 128, WIDE), BF16),
         pltpu.VMEM((1, 1, 128), F32),
         pltpu.VMEM((COUNT, 1, 128), F32),
         pltpu.VMEM((2, 4, 2, ROWS, 128), F32),
     ] + held[1:] + [
-        pltpu.SemaphoreType.DMA((10,)),
-        pltpu.SemaphoreType.DMA((10,)),
+        pltpu.SemaphoreType.DMA((15,)),
+        pltpu.SemaphoreType.DMA((15,)),
         pltpu.SemaphoreType.DMA((3,)),
         pltpu.SemaphoreType.DMA((3,)),
         pltpu.SemaphoreType.DMA((19,)),

time: 59.6 us -> 62.5 us (1.049)
  Pallas kernels: 54.6 us -> 57.5 us
    pallas_call x1, Pallas kernels: 54.6 us -> 57.5 us  [shards(): pl.pallas_call(flow_kernel, out_shape=(jax.ShapeDtypeStruct((16, 1, 32, 1...]
where the time goes in v4:
time: 62.5 us; the launch traced here: 62.3 us
  Pallas kernels  57.5 us (92%)
  local copies, waits for them, and re-layouts  2.42 us (4%)
  between operations  2.42 us (4%)
    pallas_call x1, Pallas kernels, shards(): pl.pallas_call(flow_kernel, out_shape=(jax.ShapeDtypeStruct((16, 1, 32, 1...  57.5 us
    unnamed x4, local copies, waits for them, and re-layouts  2.42 us

profile of v4, /device:TPU:1, one launch (start us, length us, event | category | flops | bytes accessed | tf_op | source)
XLA Modules:
  0.0 62.3 jit_solution(8679650087658346508)
XLA Ops:
  0.6 57.5 %flow.1 = (f32[16,1,32,128]{3,2,1,0:T(8,128)}, f32[16,1,32,128]{3,2,1,0:T(8,128)}, f32[1,1]{1,0:T(1,128)}) custom-call(f32[4,2,64,256]{3,2,1,0:T(8,128)} %dens_hbm.1, bf16[54,128]{1,0:T(8,128)(2,1)} %first_w_hbm.1, f32[1,128]{1,0:T(1,128)} %bitcast.5, bf16[128,128]{1,0:T(8,128)(2,1)} %middle_w_hbm.1, f32[1,128]{1,0:T(1,128)} %bitcast.6, ...), custom_call_target="tpu_custom_call" | custom-call | tf_op jit(solution)/shard_map/flow/pallas_call | solution.py:663
  58.2 0.0 copy-start
  58.2 1.7 %copy.22 = f32[16,1,32,128]{3,2,1,0:T(8,128)} copy(f32[16,1,32,128]{3,2,1,0:T(8,128)} %get-tuple-element.12) | data formatting | bytes 524288
  59.9 0.0 copy-done
  59.9 0.7 %copy.23 = f32[16,1,32,128]{3,2,1,0:T(8,128)} copy(f32[16,1,32,128]{3,2,1,0:T(8,128)S(1)} %copy-done) | data formatting | bytes 524288
Async XLA Ops:
  58.2 1.7 %copy-start = (f32[16,1,32,128]{3,2,1,0:T(8,128)S(1)}, f32[16,1,32,128]{3,2,1,0:T(8,128)}, u32[]{:S(2)}) copy-start(f32[16,1,32,128]{3,2,1,0:T(8,128)} %get-tuple-element.13) | copy-start | bytes 786436

commit v5 on v4

--- a/solution.py
+++ b/solution.py
@@ -428,9 +428,8 @@
         middle(0)
         first(1)
 
-    def run_groups(first, middle, last, begin, end, beside=lambda group: None):
+    def run_groups(first, middle, last, begin, end):
         def step(group, carry):
-            beside(group)
             last(group - 2)
             middle(group - 1)
             first(group)
@@ -514,12 +513,12 @@
             recv_sem=all_rsem.at[stage], device_id=to, device_id_type=LOGICAL,
         ).start()
 
-    def send_all(part, dst, stage, end=COUNT):
+    def send_all(part, dst, stage):
         def one(i, carry):
             send_one(part, dst, stage, i)
             return carry
 
-        lax.fori_loop(1, end, one, 0)
+        lax.fori_loop(1, COUNT, one, 0)
         dst[me] = part(me)[...]
 
     def wait_all(dst, stage):
@@ -534,20 +533,12 @@
     def x_part(to):
         return x_send.at[to]
 
-    each = (COUNT - 1) // (GROUPS - 2)
-    before = COUNT - each * (GROUPS - 2)
-
-    def send_some(group):
-        for i in range(each):
-            send_one(x_part, z_recv, 0, before + (group - 2) * each + i)
-
-    send_all(x_part, z_recv, 0, before)
+    send_all(x_part, z_recv, 0)
     far_plane.wait_recv()
     for c in range(2):
         put(2, ROWS, c, jnp.where(has_prev, lower_prev[0, c].astype(F32), 0.0))
     start_groups(*early)
-    run_groups(*early, 2, GROUPS, send_some)
-    end_groups(*early)
+    run_groups(*early, 2, 6)
     kept[1], scale_sum = couple(acc1, 1, 1)
     total = total + fold(scale_sum)
     wait_all(z_recv, 0)
@@ -574,6 +565,8 @@
 
     send_all(lambda to: zb_send.at[to // GY, lax.rem(to, GY)], x_recv, 1)
 
+    run_groups(*early, 6, GROUPS)
+    end_groups(*early)
     squares_sum = fold(kept[0] * kept[0])
     for parity in range(2):
         coupled, scale_sum = couple(acc0, 0, parity)
@@ -660,6 +653,7 @@
         pltpu.SemaphoreType.DMA((3,)),
         pltpu.SemaphoreType.DMA((19,)),
     ]
+    operands = [pltpu.with_memory_space_constraint(value, pltpu.HBM) for value in operands]
     factored, latent, log_density = pl.pallas_call(
         flow_kernel,
         out_shape=(
@@ -671,7 +665,7 @@
         out_specs=(vmem, vmem, smem),
         scratch_shapes=buffers,
         compiler_params=pltpu.CompilerParams(
-            collective_id=0, has_side_effects=True, vmem_limit_bytes=60 * 1024 * 1024
+            collective_id=0, has_side_effects=True, vmem_limit_bytes=52 * 1024 * 1024
         ),
         name="flow",
     )(*operands)

time: 62.5 us -> 57.1 us (0.914)
  Pallas kernels: 57.5 us -> 53.1 us
  local copies, waits for them, and re-layouts: 2.42 us -> 1.41 us
    pallas_call x1, Pallas kernels: 57.5 us -> 53.1 us  [shards(): pl.pallas_call(flow_kernel, out_shape=(jax.ShapeDtypeStruct((16, 1, 32, 1...]
    unnamed x4 -> x2, local copies, waits for them, and re-layouts: 2.42 us -> 1.41 us
where the time goes in v5:
time: 57.1 us; the launch traced here: 56.9 us
  Pallas kernels  53.1 us (93%)
  between operations  2.33 us (4%)
  local copies, waits for them, and re-layouts  1.41 us (2%)
    pallas_call x1, Pallas kernels, shards(): pl.pallas_call(flow_kernel, out_shape=(jax.ShapeDtypeStruct((16, 1, 32, 1...  53.1 us
    unnamed x2, local copies, waits for them, and re-layouts  1.41 us

profile of v5, /device:TPU:1, one launch (start us, length us, event | category | flops | bytes accessed | tf_op | source)
XLA Modules:
  0.0 56.9 jit_solution(13281363933026394604)
XLA Ops:
  0.6 53.1 %flow.1 = (f32[16,1,32,128]{3,2,1,0:T(8,128)S(1)}, f32[16,1,32,128]{3,2,1,0:T(8,128)S(1)}, f32[1,1]{1,0:T(1,128)}) custom-call(f32[4,2,64,256]{3,2,1,0:T(8,128)} %dens_hbm.1, bf16[54,128]{1,0:T(8,128)(2,1)} %first_w_hbm.1, f32[1,128]{1,0:T(1,128)} %bitcast.5, bf16[128,128]{1,0:T(8,128)(2,1)} %middle_w_hbm.1, f32[1,128]{1,0:T(1,128)} %bitcast.6, ...), custom_call_target="tpu_custom_call" | custom-call | tf_op jit(solution)/shard_map/flow/pallas_call | solution.py:657
  53.8 0.7 %copy.22 = f32[16,1,32,128]{3,2,1,0:T(8,128)} copy(f32[16,1,32,128]{3,2,1,0:T(8,128)S(1)} %get-tuple-element.12) | data formatting | bytes 524288
  54.5 0.7 %copy.23 = f32[16,1,32,128]{3,2,1,0:T(8,128)} copy(f32[16,1,32,128]{3,2,1,0:T(8,128)S(1)} %get-tuple-element.13) | data formatting | bytes 524288

commit v6 on v5

--- a/solution.py
+++ b/solution.py
@@ -24,7 +24,7 @@
 OWN_ROWS = ROWS + 2
 CHUNK = 16
 CHUNKS = ROWS // CHUNK
-GROUP = 6
+GROUP = 11
 GROUPS = OWN_ROWS // GROUP
 
 
@@ -99,8 +99,19 @@
     return lax.dot_general(a, b, (dims, ((), ())), preferred_element_type=F32)
 
 
-def mul3(a, b, dims=((1,), (0,))):
-    return mul(a[0], b[0], dims) + (mul(a[0], b[1], dims) + mul(a[1], b[0], dims))
+def table_times(table, values):
+    high, low = split2(values)
+    columns = values.shape[1]
+    both = mul(table[0], jnp.concatenate([high, low], axis=1))
+    return both[:, :columns] + (both[:, columns:] + mul(table[1], high))
+
+
+def times_table(values, table, turned=False):
+    dims = ((1,), (1,)) if turned else ((1,), (0,))
+    high, low = split2(values)
+    rows = values.shape[0]
+    both = mul(jnp.concatenate([high, low], axis=0), table[0], dims)
+    return both[:rows] + (both[rows:] + mul(high, table[1], dims))
 
 
 def shift_right(values):
@@ -305,7 +316,7 @@
         kappa = jnp.sqrt(squares[:, lanes] + freq_x * freq_x) * (2.0 / math.sqrt(3.0))
         scaled = kappa * 31.0 - centres
         basis = jnp.exp(-scaled * scaled)
-        values = mul3(split2(weights), split2(basis))
+        values = table_times(split2(weights), basis)
         for j in range(4):
             profile[pl.ds(part * 4 + j, 128, stride=32), :] = values[:, j * 128 : (j + 1) * 128]
         return carry
@@ -445,15 +456,15 @@
     later = (later_first, later_second, later_last)
     early = (early_first, early_second, early_last)
 
-    start_groups(*later)
+    later_first(0)
     fill_edge(1)
-
-    def later_chunk(chunk, carry):
-        fill_chunk(chunk)
-        run_groups(*later, 3 * chunk - 1, 3 * chunk + 2)
-        return carry
-
-    lax.fori_loop(1, CHUNKS, later_chunk, 0)
+    fill_chunk(1)
+    later_second(0)
+    later_first(1)
+    fill_chunk(2)
+    run_groups(*later, 2, 4)
+    fill_chunk(3)
+    run_groups(*later, 4, GROUPS)
     end_groups(*later)
 
     def couple(acc, z, parity):
@@ -499,9 +510,9 @@
     source, scale_sum = couple(acc1, 1, 0)
     kept[0] = source
     total = fold(scale_sum)
-    x_modes = mul3(
-        (forward_x[0], forward_x[1]), split2(source), ((1,), (1,))
-    )
+    high, low = split2(source)
+    both = mul(forward_x[0], jnp.concatenate([high, low], axis=0), ((1,), (1,)))
+    x_modes = both[:, :128] + (both[:, 128:] + mul(forward_x[1], high, ((1,), (1,))))
     x_send[...] = x_modes.reshape(COUNT, 2, 128)
 
     sent = list(halo)
@@ -538,15 +549,15 @@
     for c in range(2):
         put(2, ROWS, c, jnp.where(has_prev, lower_prev[0, c].astype(F32), 0.0))
     start_groups(*early)
-    run_groups(*early, 2, 6)
+    run_groups(*early, 2, 4)
     kept[1], scale_sum = couple(acc1, 1, 1)
     total = total + fold(scale_sum)
     wait_all(z_recv, 0)
 
-    z_modes = mul3((forward_z[0], forward_z[1]), split2(z_recv[...].reshape(256, 128)))
+    z_modes = table_times(forward_z, z_recv[...].reshape(256, 128))
 
     lines = jnp.concatenate([z_modes[g * 64 : (g + 1) * 64] for g in range(GY)], axis=1)
-    modes = mul3(split2(lines), (forward_y[0], forward_y[1]))
+    modes = times_table(lines, forward_y)
     parts = [
         modes[k * 32 : (k + 1) * 32, c * 128 : (c + 1) * 128] for k in range(2) for c in range(4)
     ]
@@ -555,17 +566,24 @@
         for c in range(1, 8):
             value = value + profile[pl.ds(o * 256 + c * 32, 32), :] * parts[c]
         mixed[pl.ds((o // 4) * 32, 32), pl.ds((o % 4) * 128, 128)] = value
-    back = mul3(split2(mixed[...]), (forward_y[0], forward_y[1]), ((1,), (1,)))
+    back = times_table(mixed[...], forward_y, turned=True)
+    lines = jnp.concatenate(
+        [
+            jnp.concatenate(
+                [back[:, g * 128 : (g + 1) * 128] for g in (2 * pair, 2 * pair + 1)], axis=0
+            )
+            for pair in range(2)
+        ],
+        axis=1,
+    )
+    planes = table_times(backward_z, lines)
     for pair in range(2):
-        lines = jnp.concatenate(
-            [back[:, g * 128 : (g + 1) * 128] for g in (2 * pair, 2 * pair + 1)], axis=0
-        )
-        planes = mul3((backward_z[0], backward_z[1]), split2(lines))
-        zb_send[:, pl.ds(pair * 2, 2)] = planes.reshape(GZ, 2, 4, 128)
+        part = planes[:, pair * 128 : (pair + 1) * 128]
+        zb_send[:, pl.ds(pair * 2, 2)] = part.reshape(GZ, 2, 4, 128)
 
     send_all(lambda to: zb_send.at[to // GY, lax.rem(to, GY)], x_recv, 1)
 
-    run_groups(*early, 6, GROUPS)
+    run_groups(*early, 4, GROUPS)
     end_groups(*early)
     squares_sum = fold(kept[0] * kept[0])
     for parity in range(2):
@@ -576,10 +594,9 @@
     target = spread_x(kept[1])
     wait_all(x_recv, 1)
 
-    shifts = []
-    for og in range(4):
-        lines = x_recv[:, og, :]
-        shifts.append(jnp.transpose(mul3((backward_x[0], backward_x[1]), split2(lines))))
+    lines = jnp.concatenate([x_recv[:, og, :] for og in range(4)], axis=1)
+    moved = table_times(backward_x, lines)
+    shifts = [jnp.transpose(moved[:, og * 128 : (og + 1) * 128]) for og in range(4)]
     for k in range(2):
         scale = jnp.tanh(shifts[k])
         total = total + fold(scale)

time: 57.1 us -> 55.8 us (0.977)
  Pallas kernels: 53.1 us -> 51.9 us
    pallas_call x1, Pallas kernels: 53.1 us -> 51.9 us  [shards(): pl.pallas_call(flow_kernel, out_shape=(jax.ShapeDtypeStruct((16, 1, 32, 1...]
where the time goes in v6:
time: 55.8 us; the launch traced here: 55.6 us
  Pallas kernels  51.9 us (93%)
  between operations  2.33 us (4%)
  local copies, waits for them, and re-layouts  1.41 us (3%)
    pallas_call x1, Pallas kernels, shards(): pl.pallas_call(flow_kernel, out_shape=(jax.ShapeDtypeStruct((16, 1, 32, 1...  51.9 us
    unnamed x2, local copies, waits for them, and re-layouts  1.41 us

profile of v6, /device:TPU:1, one launch (start us, length us, event | category | flops | bytes accessed | tf_op | source)
XLA Modules:
  0.0 55.6 jit_solution(1537024216699737118)
XLA Ops:
  0.6 51.9 %flow.1 = (f32[16,1,32,128]{3,2,1,0:T(8,128)S(1)}, f32[16,1,32,128]{3,2,1,0:T(8,128)S(1)}, f32[1,1]{1,0:T(1,128)}) custom-call(f32[4,2,64,256]{3,2,1,0:T(8,128)} %dens_hbm.1, bf16[54,128]{1,0:T(8,128)(2,1)} %first_w_hbm.1, f32[1,128]{1,0:T(1,128)} %bitcast.5, bf16[128,128]{1,0:T(8,128)(2,1)} %middle_w_hbm.1, f32[1,128]{1,0:T(1,128)} %bitcast.6, ...), custom_call_target="tpu_custom_call" | custom-call | tf_op jit(solution)/shard_map/flow/pallas_call | solution.py:674
  52.5 0.7 %copy.22 = f32[16,1,32,128]{3,2,1,0:T(8,128)} copy(f32[16,1,32,128]{3,2,1,0:T(8,128)S(1)} %get-tuple-element.12) | data formatting | bytes 524288
  53.3 0.7 %copy.23 = f32[16,1,32,128]{3,2,1,0:T(8,128)} copy(f32[16,1,32,128]{3,2,1,0:T(8,128)S(1)} %get-tuple-element.13) | data formatting | bytes 524288

commit v7 on v6

--- a/solution.py
+++ b/solution.py
@@ -136,7 +136,7 @@
     kept, first_held, last_held, sum_send, sum_recv, dens2,
     first_w, first_b, middle_w, middle_b, output_w, output_b,
     radial, forward_x, forward_z, backward_z, forward_y, backward_x, spread, pick, squares,
-    halo_ssem, halo_rsem, all_ssem, all_rsem, in_sem,
+    halo_ssem, halo_rsem, all_ssem, all_rsem, in_sem, known,
 ):
     me_z = lax.axis_index("gz")
     me_y = lax.axis_index("gy")
@@ -170,12 +170,6 @@
         )
         for half in range(2)
     ]
-
-    def greet(i, carry):
-        pl.semaphore_signal(barrier, inc=1, device_id=near(i), device_id_type=LOGICAL)
-        return carry
-
-    lax.fori_loop(1, COUNT, greet, 0)
 
     for copy in lower_in:
         copy.wait()
@@ -194,8 +188,20 @@
                             side, pl.ds(row * 4 + z * 2 + c, 1), pl.ds(half * 128, 128)
                         ] = line.astype(BF16).astype(F32)
 
-    pl.semaphore_wait(barrier, COUNT - 1 + len(sides))
-
+    pl.semaphore_wait(barrier, len(sides))
+
+    reach = [sides, [(-2, 0), (2, 0)], [(-4, 0), (4, 0)], [(-8, 0), (8, 0)]]
+
+    def tell(turn):
+        for dz, dy in reach[turn]:
+            pl.semaphore_signal(
+                known.at[turn], inc=1, device_id=(near_z(dz), near_y(dy)), device_id_type=MESH
+            )
+
+    def hear(turn):
+        pl.semaphore_wait(known.at[turn], len(reach[turn]))
+
+    tell(0)
     halo = []
 
     def halo_copy(src, dst, index, to):
@@ -362,6 +368,8 @@
                             :, half * 128 : (half + 1) * 128
                         ]
 
+    hear(0)
+    tell(1)
     fill_edge(0)
     fill_chunk(0)
 
@@ -462,10 +470,15 @@
     later_second(0)
     later_first(1)
     fill_chunk(2)
+    hear(1)
+    tell(2)
     run_groups(*later, 2, 4)
     fill_chunk(3)
+    hear(2)
+    tell(3)
     run_groups(*later, 4, GROUPS)
     end_groups(*later)
+    hear(3)
 
     def couple(acc, z, parity):
         raw = []
@@ -669,6 +682,7 @@
         pltpu.SemaphoreType.DMA((3,)),
         pltpu.SemaphoreType.DMA((3,)),
         pltpu.SemaphoreType.DMA((19,)),
+        pltpu.SemaphoreType.REGULAR((4,)),
     ]
     operands = [pltpu.with_memory_space_constraint(value, pltpu.HBM) for value in operands]
     factored, latent, log_density = pl.pallas_call(

time: 55.8 us -> 55 us (0.986)
  Pallas kernels: 51.9 us -> 51.1 us
    pallas_call x1, Pallas kernels: 51.9 us -> 51.1 us  [shards(): pl.pallas_call(flow_kernel, out_shape=(jax.ShapeDtypeStruct((16, 1, 32, 1...]
where the time goes in v7:
time: 55 us; the launch traced here: 54.9 us
  Pallas kernels  51.1 us (93%)
  between operations  2.33 us (4%)
  local copies, waits for them, and re-layouts  1.41 us (3%)
    pallas_call x1, Pallas kernels, shards(): pl.pallas_call(flow_kernel, out_shape=(jax.ShapeDtypeStruct((16, 1, 32, 1...  51.1 us
    unnamed x2, local copies, waits for them, and re-layouts  1.41 us

profile of v7, /device:TPU:1, one launch (start us, length us, event | category | flops | bytes accessed | tf_op | source)
XLA Modules:
  0.0 54.9 jit_solution(16306455039001282779)
XLA Ops:
  0.6 51.1 %flow.1 = (f32[16,1,32,128]{3,2,1,0:T(8,128)S(1)}, f32[16,1,32,128]{3,2,1,0:T(8,128)S(1)}, f32[1,1]{1,0:T(1,128)}) custom-call(f32[4,2,64,256]{3,2,1,0:T(8,128)} %dens_hbm.1, bf16[54,128]{1,0:T(8,128)(2,1)} %first_w_hbm.1, f32[1,128]{1,0:T(1,128)} %bitcast.5, bf16[128,128]{1,0:T(8,128)(2,1)} %middle_w_hbm.1, f32[1,128]{1,0:T(1,128)} %bitcast.6, ...), custom_call_target="tpu_custom_call" | custom-call | tf_op jit(solution)/shard_map/flow/pallas_call | solution.py:688
  51.8 0.7 %copy.22 = f32[16,1,32,128]{3,2,1,0:T(8,128)} copy(f32[16,1,32,128]{3,2,1,0:T(8,128)S(1)} %get-tuple-element.12) | data formatting | bytes 524288
  52.5 0.7 %copy.23 = f32[16,1,32,128]{3,2,1,0:T(8,128)} copy(f32[16,1,32,128]{3,2,1,0:T(8,128)S(1)} %get-tuple-element.13) | data formatting | bytes 524288

commit v8 on v7

--- a/solution.py
+++ b/solution.py
@@ -539,10 +539,13 @@
 
     def send_all(part, dst, stage):
         def one(i, carry):
-            send_one(part, dst, stage, i)
+            for sub in range(4):
+                send_one(part, dst, stage, 4 * i + sub)
             return carry
 
-        lax.fori_loop(1, COUNT, one, 0)
+        for step in range(1, 4):
+            send_one(part, dst, stage, step)
+        lax.fori_loop(1, COUNT // 4, one, 0)
         dst[me] = part(me)[...]
 
     def wait_all(dst, stage):

time: 55 us -> 54.2 us (0.985)
  Pallas kernels: 51.1 us -> 50.3 us
    pallas_call x1, Pallas kernels: 51.1 us -> 50.3 us  [shards(): pl.pallas_call(flow_kernel, out_shape=(jax.ShapeDtypeStruct((16, 1, 32, 1...]
where the time goes in v8:
time: 54.2 us; the launch traced here: 54 us
  Pallas kernels  50.3 us (93%)
  between operations  2.33 us (4%)
  local copies, waits for them, and re-layouts  1.41 us (3%)
    pallas_call x1, Pallas kernels, shards(): pl.pallas_call(flow_kernel, out_shape=(jax.ShapeDtypeStruct((16, 1, 32, 1...  50.3 us
    unnamed x2, local copies, waits for them, and re-layouts  1.41 us

profile of v8, /device:TPU:1, one launch (start us, length us, event | category | flops | bytes accessed | tf_op | source)
XLA Modules:
  0.0 54.0 jit_solution(14300350012998834491)
XLA Ops:
  0.6 50.3 %flow.1 = (f32[16,1,32,128]{3,2,1,0:T(8,128)S(1)}, f32[16,1,32,128]{3,2,1,0:T(8,128)S(1)}, f32[1,1]{1,0:T(1,128)}) custom-call(f32[4,2,64,256]{3,2,1,0:T(8,128)} %dens_hbm.1, bf16[54,128]{1,0:T(8,128)(2,1)} %first_w_hbm.1, f32[1,128]{1,0:T(1,128)} %bitcast.5, bf16[128,128]{1,0:T(8,128)(2,1)} %middle_w_hbm.1, f32[1,128]{1,0:T(1,128)} %bitcast.6, ...), custom_call_target="tpu_custom_call" | custom-call | tf_op jit(solution)/shard_map/flow/pallas_call | solution.py:691
  50.9 0.7 %copy.22 = f32[16,1,32,128]{3,2,1,0:T(8,128)} copy(f32[16,1,32,128]{3,2,1,0:T(8,128)S(1)} %get-tuple-element.12) | data formatting | bytes 524288
  51.6 0.7 %copy.23 = f32[16,1,32,128]{3,2,1,0:T(8,128)} copy(f32[16,1,32,128]{3,2,1,0:T(8,128)S(1)} %get-tuple-element.13) | data formatting | bytes 524288
